TPU v7x, 128 devices: a whole 4x4x4 slice. The times are simulated.
128 devices in a mesh: rows: 4 (over y), cols: 32 (over z, x, core).
Axes of the slice: x: 4, y: 4, z: 4, core: 2. Of those that a mesh axis runs over, the one named last changes fastest.
Arguments:
- sigma_in: bfloat16 [2048, 32768], P('rows', 'cols'), may hold values from -6 to 6
- theta_in: bfloat16 [2048, 32768], P('rows', 'cols'), may hold values from -6 to 6
- var_rows: float32 [2048], P('rows'), may hold values from 0.3 to 3
- var_cols: float32 [32768], P('cols'), may hold values from 0.3 to 3
- row_nbrs: int32 [8, 3], replicated, may hold values from 0 to 7, as said below
- row_vals: bfloat16 [8, 3, 256, 256], replicated, may hold values from -0.21875 to 0.21875
- col_nbrs: int32 [128, 20], replicated, may hold values from 0 to 127, as said below
- col_vals: bfloat16 [128, 20, 256, 256], P('cols'), may hold values from -0.078125 to 0.078125
Outputs:
- nngp_out: float32 [2048, 32768], P('rows', 'cols')
- ntk_out: float32 [2048, 32768], P('rows', 'cols')
Inputs may be any that keep to these rules, and one draw needn't show every extreme that they name: `row_nbrs`: the 3 entries of one row are distinct. `col_nbrs`: column block c belongs to index c // 4 of cols. The lists of the 4 column blocks of one index of cols name, of each other index of cols, at most one block (possibly several times).
All inputs are finite; a program needn't handle non-finite values.
Results may differ from a plain program's by a relative error of at most 0.0026.
Values may be sent and summed in bfloat16 or wider, within the bound.
A program may use at most 256 MiB of HBM per device.

v0:
```python
import jax
import jax.numpy as jnp
from jax import lax
from jax.sharding import PartitionSpec as P


def shards(sigma_in, theta_in, var_rows, var_cols, row_nbrs, row_vals, col_nbrs, col_vals):
    block_size = row_vals.shape[2]
    rows_dev = sigma_in.shape[0]
    cols_dev = sigma_in.shape[1]
    blocks_dev = cols_dev // block_size
    list_length = col_nbrs.shape[1]
    panel_blocks = row_nbrs.shape[0]
    panel_rows = panel_blocks * block_size
    rank_row = lax.axis_index("rows")
    rank_col = lax.axis_index("cols")
    col_devices = lax.axis_size("cols")
    selector = (
        row_nbrs[:, :, None] == jnp.arange(panel_blocks, dtype=jnp.int32)[None, None, :]
    ).astype(jnp.bfloat16)
    left_full = jnp.einsum("pkq,pkij->piqj", selector, row_vals, preferred_element_type=jnp.float32)
    left_full = left_full.astype(jnp.bfloat16).reshape(panel_rows, panel_rows)
    paired = jnp.stack(
        [
            sigma_in.reshape(rows_dev, blocks_dev, block_size),
            theta_in.reshape(rows_dev, blocks_dev, block_size),
        ],
        axis=2,
    )
    paired = paired.reshape(rows_dev, 2 * cols_dev)
    own_columns = lax.dynamic_slice_in_dim(left_full, rank_row * rows_dev, rows_dev, 1)
    summed = lax.psum_scatter(
        jnp.dot(own_columns, paired, preferred_element_type=jnp.float32),
        "rows",
        scatter_dimension=0,
        tiled=True,
    )
    aggregated = summed.astype(jnp.bfloat16)
    local_blocks = aggregated.reshape(rows_dev, blocks_dev, 2 * block_size)
    owners = col_nbrs // blocks_dev
    within = col_nbrs % blocks_dev
    mine = (owners == rank_col).reshape(col_devices, blocks_dev * list_length)
    wanted = jnp.max(
        jnp.where(mine, within.reshape(col_devices, blocks_dev * list_length) + 1, 0), axis=1
    )
    wanted = jnp.where(jnp.arange(col_devices, dtype=jnp.int32) == rank_col, 0, wanted)
    picker = (wanted[:, None] == jnp.arange(1, blocks_dev + 1, dtype=jnp.int32)[None, :]).astype(
        jnp.bfloat16
    )
    send_slots = jnp.einsum(
        "eb,rbx->rex", picker, local_blocks, preferred_element_type=jnp.float32
    ).astype(jnp.bfloat16)
    arrived = lax.all_to_all(send_slots, "cols", split_axis=1, concat_axis=1, tiled=True)
    source_pool = jnp.concatenate([local_blocks, arrived], axis=1)
    my_nbrs = lax.dynamic_slice_in_dim(col_nbrs, rank_col * blocks_dev, blocks_dev, 0)
    my_owner = my_nbrs // blocks_dev
    pool_index = jnp.where(my_owner == rank_col, my_nbrs % blocks_dev, blocks_dev + my_owner)
    sources = jnp.take(source_pool, pool_index.reshape(-1), axis=1)
    sources = sources.reshape(rows_dev, blocks_dev, list_length, 2, block_size)
    combined = jnp.einsum("rcksj,ckij->srci", sources, col_vals, preferred_element_type=jnp.float32)
    combined = combined.reshape(2, rows_dev, cols_dev)
    agg_sigma = combined[0]
    agg_theta = combined[1]
    scale_rc = jnp.sqrt(var_rows[:, None] * var_cols[None, :])
    hypotenuse = jnp.sqrt(scale_rc * scale_rc + agg_sigma * agg_sigma)
    correlation = agg_sigma / hypotenuse
    arc_angle = jnp.arccos(correlation)
    nngp_out = scale_rc / jnp.pi * (scale_rc / hypotenuse + (jnp.pi - arc_angle) * correlation)
    ntk_out = nngp_out + agg_theta * (jnp.pi - arc_angle) / jnp.pi
    return (nngp_out, ntk_out)


def solution(mesh):
    in_specs = (
        P("rows", "cols"),
        P("rows", "cols"),
        P("rows"),
        P("cols"),
        P(),
        P(),
        P(),
        P("cols", None, None, None),
    )
    out_specs = (P("rows", "cols"), P("rows", "cols"))
    return jax.shard_map(shards, mesh=mesh, in_specs=in_specs, out_specs=out_specs, check_vma=False)
```

profile of v0, /device:TPU:0, one launch (start us, length us, event | category | flops | bytes accessed | tf_op | source)
XLA Modules:
  0.0 590.3 jit_solution(157447862003336327)
XLA Ops:
  7.2 0.9 copy.45
  8.1 2.3 copy.47
  10.4 2.3 copy.48
  12.7 5.8 convolution_convert_fusion
  18.4 10.4 %copy.61 = bf16[256,8,8,256]{3,1,2,0:T(8,128)(2,1)} copy(bf16[256,8,8,256]{3,2,1,0:T(8,128)(2,1)} %bitcast.43) | data formatting | bytes 16777216
  28.9 0.2 pad_maximum_fusion.1
  29.1 9.8 %fusion.8 = f32[2048,2048]{1,0:T(8,128)} fusion(bf16[512,2048]{0,1:T(8,128)(2,1)S(1)} %bitcast.51, bf16[2048,2048]{1,0:T(8,128)(2,1)} %bitcast.46, s32[]{:T(128)S(6)} %select_n.72), kind=kOutput, calls=%fused_computation.17 | convolution fusion | flops 4294967296 | bytes 20971524 | tf_op jit(solution)/shard_map/dot_general | solution.py:33
  38.9 0.7 copy-done.4
  39.9 149.6 %reduce-scatter.2.cloned.1.call-done = f32[512,2048]{1,0:T(8,128)} async-done(((f32[2048,2048]{1,0:T(8,128)}), f32[512,2048]{1,0:T(8,128)}) %reduce-scatter.2.cloned.1.call-update) | async-done | bytes 4194320 | tf_op jit(solution)/shard_map/reduce_scatter | solution.py:32
  189.5 2.5 convert_element_type.19
  192.0 2.8 reshape.77
  194.8 11.9 %convert_bitcast_fusion = bf16[512,32,512]{2,1,0:T(8,128)(2,1)} fusion(bf16[512,4,512]{2,1,0:T(4,128)(2,1)} %reshape.77, s32[32]{0:T(128)S(1)} %compare_select_fusion.2, s32[4]{0:T(128)S(1)} %iota_add_fusion), kind=kOutput, calls=%fused_computation.6 | convolution fusion | flops 75497600 | bytes 18874512 | tf_op jit(solution)/shard_map/eb,rbx->rex/dot_general | solution.py:50
  206.7 16.8 %copy.49 = bf16[512,32,512]{2,0,1:T(8,128)(2,1)} copy(bf16[512,32,512]{2,1,0:T(8,128)(2,1)} %convert_bitcast_fusion) | data formatting | bytes 33554432 | tf_op jit(solution)/shard_map/convert_element_type | solution.py:52
  223.5 7.6 %all-to-all-start = ((bf16[512,32,512]{2,0,1:T(8,128)(2,1)}), bf16[512,32,512]{2,0,1:T(8,128)(2,1)}, u32[]{:S(2)}, u32[]{:S(2)}) async-start(bf16[512,32,512]{2,0,1:T(8,128)(2,1)} %copy.49), calls=%async_computation.1 | async-start | bytes 33554432 | tf_op jit(solution)/shard_map/all_to_all | solution.py:53
  231.4 1.5 copy.69
  232.9 211.2 %all-to-all-done = bf16[512,32,512]{2,0,1:T(8,128)(2,1)} async-done(((bf16[512,32,512]{2,0,1:T(8,128)(2,1)}), bf16[512,32,512]{2,0,1:T(8,128)(2,1)}, u32[]{:S(2)}, u32[]{:S(2)}) %all-to-all-start) | async-done | bytes 16777248 | tf_op jit(solution)/shard_map/all_to_all | solution.py:53
  444.1 16.1 %pad_maximum_fusion = bf16[512,36,512]{2,0,1:T(8,128)(2,1)} fusion(bf16[512,32,512]{2,0,1:T(8,128)(2,1)} %all-to-all-done, bf16[512,4,512]{2,0,1:T(8,128)(2,1)} %bitcast.45), kind=kLoop, calls=%fused_computation.5 | loop fusion | flops 9437184 | bytes 37748736 | tf_op jit(solution)/shard_map/concatenate | solution.py:54
  460.2 21.4 %gather_fusion = bf16[80,512,512]{2,1,0:T(8,128)(2,1)} fusion(bf16[512,36,512]{2,0,1:T(8,128)(2,1)} %pad_maximum_fusion, s32[1024]{0:T(1024)S(1)} %pad_clamp_fusion), kind=kCustom, calls=%fused_computation | custom fusion | bytes 83886400 | tf_op jit(solution)/shard_map/jit(_take)/gather | solution.py:58
  481.5 57.4 %gather.7 = bf16[512,4,20,2,256]{4,3,0,2,1:T(2,128)(2,1)} reshape(bf16[512,80,512]{2,0,1:T(8,128)(2,1)} %bitcast.42) | data formatting | bytes 83886080 | tf_op jit(solution)/shard_map/jit(_take)/gather | solution.py:58
  538.9 25.7 %fusion.5 = f32[2,512,4,256]{1,3,0,2:T(8,128)} fusion(bf16[4,20,256,256]{3,2,1,0:T(8,128)(2,1)} %param.15, bf16[512,4,20,2,256]{4,3,0,2,1:T(2,128)(2,1)} %gather.7, pred[4,20]{1,0:T(4,128)(4,1)S(1)} %get-tuple-element.4), kind=kOutput, calls=%fused_computation.10 | convolution fusion | flops 10758389760 | bytes 56623184 | tf_op jit(solution)/shard_map/rcksj,ckij->srci/dot_general | solution.py:60
  564.6 4.0 fusion.30
  568.6 2.9 copy.52
  571.5 1.8 copy.55
  573.3 10.2 %multiply_add_fusion = (f32[512,1024]{1,0:T(8,128)}, f32[512,1024]{1,0:T(8,128)}) fusion(f32[512,1024]{1,0:T(8,128)} %copy.55, f32[512,1024]{1,0:T(8,128)} %copy.52, f32[1024]{0:T(1024)S(1)} %copy-done.5, f32[512]{0:T(512)S(1)} %copy-done.6), kind=kLoop, calls=%fused_computation.13 | loop fusion | flops 8912896 | bytes 8394752 | tf_op jit(solution)/shard_map/add | solution.py:69
  (26 shorter events, 0.6 us)
Async XLA Ops:
  7.2 5.5 copy-start
  7.2 182.3 %reduce-scatter.2.cloned.1.call-start = ((), (), s32[]{:S(2)}) async-start(), calls=%async_computation.2 | async-start | bytes 20971520 | tf_op jit(solution)/shard_map/reduce_scatter | solution.py:32
  18.4 10.4 %copy-start.2 = (bf16[512,1024]{0,1:T(8,128)(2,1)S(1)}, bf16[512,1024]{0,1:T(8,128)(2,1)}, u32[]{:S(2)}) copy-start(bf16[512,1024]{0,1:T(8,128)(2,1)} %copy.47) | copy-start | bytes 3145732
  18.4 10.4 %copy-start.3 = (bf16[512,1024]{0,1:T(8,128)(2,1)S(1)}, bf16[512,1024]{0,1:T(8,128)(2,1)}, u32[]{:S(2)}) copy-start(bf16[512,1024]{0,1:T(8,128)(2,1)} %copy.48) | copy-start | bytes 3145732
  38.9 0.7 copy-start.4
  223.5 220.6 %all-to-all-start = ((bf16[512,32,512]{2,0,1:T(8,128)(2,1)}), bf16[512,32,512]{2,0,1:T(8,128)(2,1)}, u32[]{:S(2)}, u32[]{:S(2)}) async-start(bf16[512,32,512]{2,0,1:T(8,128)(2,1)} %copy.49), calls=%async_computation.1 | async-start | bytes 33554432 | tf_op jit(solution)/shard_map/all_to_all | solution.py:53
  571.5 1.8 copy-start.5
  571.5 1.8 copy-start.6
  573.3 10.2 %copy-start.1 = (bf16[8,3,256,256]{3,2,1,0:T(8,128)(2,1)S(1)}, bf16[8,3,256,256]{3,2,1,0:T(8,128)(2,1)}, u32[]{:S(2)}) copy-start(bf16[8,3,256,256]{3,2,1,0:T(8,128)(2,1)} %param.13) | copy-start | bytes 9437188
Sparse Core Ops, SparseCore 0:
  39.0 150.4 reduce-scatter.1
where the time goes:
time: 592 us; the launch traced here: 590 us
  waiting for transfers between devices  361 us (61%)
  local copies, waits for them, and re-layouts  125 us (21%)
  matrix products  53.2 us (9%)
  other arithmetic  29.2 us (5%)
  between operations  14.1 us (2%)
  starting transfers between devices  7.61 us (1%)
    all_to_all x1, waiting for transfers between devices, shards(): lax.all_to_all(send_slots, 'cols', split_axis=1, concat_axis=1, tiled=True)  211 us
    reduce_scatter x1, waiting for transfers between devices, shards(): lax.psum_scatter(jnp.dot(own_columns, paired, preferred_element_type=jnp....  150 us
    gather x2, local copies, waits for them, and re-layouts, shards(): sources = jnp.take(source_pool, pool_index.reshape(-1), axis=1)  78.7 us
    dot_general x1, matrix products, shards(): jnp.einsum('rcksj,ckij->srci', sources, col_vals, preferred_element_type=...  25.7 us
    convert_element_type x1, local copies, waits for them, and re-layouts, shards(): send_slots = jnp.einsum('eb,rbx->rex', picker, local_blocks, preferred_el...  16.8 us
    unnamed x19, local copies, waits for them, and re-layouts  16.7 us
    concatenate x1, other arithmetic, shards(): source_pool = jnp.concatenate([local_blocks, arrived], axis=1)  16.1 us
    dot_general x1, matrix products, shards(): jnp.einsum('eb,rbx->rex', picker, local_blocks, preferred_element_type=jn...  11.9 us
  transfers between devices with their start and end apart: 2, of which 2 were waited for; matrix products, arithmetic and copies ran while one was open for 0% of the time, Pallas kernels for 0%

commit v1 on v0

v1 whole, which is shorter than its diff:
```python
import functools
import math

import jax
import jax.numpy as jnp
from jax import lax
from jax.experimental import pallas as pl
from jax.experimental.pallas import tpu as pltpu
from jax.sharding import PartitionSpec as P

MESH = pl.DeviceIdType.MESH
BF16 = jnp.bfloat16
F32 = jnp.float32

ATAN = (
    0.9999998979,
    -0.3333196033,
    0.1996924122,
    -0.1401660921,
    0.09906147193,
    -0.05936764426,
    0.02416647519,
    -0.004668829048,
)


def arc(t):
    t2 = t * t
    total = jnp.full_like(t, ATAN[-1])
    for c in ATAN[-2::-1]:
        total = total * t2 + c
    return total * t


def kernel(
    want, index, row_nbrs, theta, sigma, var_rows, var_cols, row_vals, col_vals,
    nngp, ntk,
    weights, row_weights, gathered_s, gathered_t, agg_theta, out_n, out_k,
    pa0, pa1, pa2, pa3, pb0, pb1, pb2, pb3,
    ra0, ra1, ra2, ra3, rb0, rb1, rb2, rb3,
    sa0, sa1, sb0, sb1,
    w_sem, rv_sem, own_sem, ys_send, ys_recv, yt_send, yt_recv,
    one_send, one_recv, two_send, two_recv, out_sem,
):
    pools = ((pa0, pb0), (pa1, pb1), (pa2, pb2), (pa3, pb3))
    slots = ((ra0, rb0), (ra1, rb1), (ra2, rb2), (ra3, rb3))
    sends = ((sa0, sb0), (sa1, sb1), (sa0, sb0), (sa1, sb1))
    y = lax.axis_index("rows")
    col = lax.axis_index("cols")
    z, x, core = col // 8, (col // 2) % 4, col % 2

    def at(dy, dz, dx, dc):
        return (
            lax.rem(y + dy, 4),
            (lax.rem(z + dz, 4) * 4 + lax.rem(x + dx, 4)) * 2 + lax.rem(core + dc, 2),
        )

    loads = []

    def load(src, dst, sem):
        copy = pltpu.make_async_copy(src, dst, sem)
        copy.start()
        loads.append(copy)
        return copy

    own_pool = {}
    for ph in range(2):
        for st in range(2):
            rows = pl.ds(ph * 256 + st * 128, 128)
            own_pool[ph, st] = [
                load(theta.at[rows, pl.ds(b * 256, 256)], pools[ph][st].at[(z, x)[st], b], own_sem.at[ph, st, b])
                for b in range(4)
            ]
    own_s = []
    for half in range(2):
        own_s.append(load(sigma.at[pl.ds(half * 256, 256)], gathered_s.at[2 * y + half], own_sem.at[2, half, 0]))

    barrier = pltpu.get_barrier_semaphore()
    partners = [(dy, 0, 0, 0) for dy in (1, 2, 3)]
    partners += [(0, dz, 0, dc) for dz in (1, 2, 3) for dc in (0, 1)]
    partners += [(0, 0, dx, dc) for dx in (1, 2, 3) for dc in (0, 1)]
    partners += [(0, 0, 0, 1)]
    for p in partners:
        pl.semaphore_signal(barrier, inc=1, device_id=at(*p), device_id_type=MESH)
    pl.semaphore_wait(barrier, len(partners))

    def line(st, d, dc):
        return at(0, d, 0, dc) if st == 0 else at(0, 0, d, dc)

    def remote(src, dst, ssem, rsem, device):
        copy = pltpu.make_async_remote_copy(
            src_ref=src, dst_ref=dst, send_sem=ssem, recv_sem=rsem, device_id=device, device_id_type=MESH
        )
        copy.start()
        return copy

    first = {}

    def stage_one(ph):
        for d in (1, 3, 2):
            for st in range(2):
                mine = (z, x)[st]
                first[ph, st, d] = remote(
                    pools[ph][st].at[mine],
                    pools[ph][st].at[mine],
                    one_send.at[ph, st, d - 1],
                    one_recv.at[ph, st, d - 1],
                    line(st, d, 0),
                )

    second = {}

    def stage_two(ph):
        for st in range(2):
            for d in (1, 2, 3):
                first[ph, st, d].wait_recv()
        for st in range(2):
            pool, out, here = pools[ph][st], sends[ph][st], slots[ph][st]
            place = (x if st == 0 else z) * 2 + core

            def source_at(s):
                return ((s * 4 + x) if st == 0 else (z * 4 + s)) * 2 + core

            if ph >= 2:
                for j in range(1, 8):
                    second[ph - 2, st, j].wait_send()

            def pack(i, carry):
                j, s = i // 4 + 1, i % 4
                d, dc = j // 2, j % 2
                other = line(1 - st, d, dc)[1]
                block = want[other * 32 + source_at(s)]
                out[j - 1, s] = pool[s, block]
                return carry

            lax.fori_loop(0, 28, pack, 0)
            for j in (2, 3, 6, 7, 4, 5, 1):
                second[ph, st, j] = remote(
                    out.at[j - 1],
                    here.at[pl.ds(place * 4, 4)],
                    two_send.at[ph, st, j - 1],
                    two_recv.at[ph, st, j - 1],
                    line(1 - st, j // 2, j % 2),
                )
        for st in range(2):
            pool, here = pools[ph][st], slots[ph][st]
            place = (x if st == 0 else z) * 2 + core
            for s in range(4):
                src = ((s * 4 + x) if st == 0 else (z * 4 + s)) * 2 + core
                block = want[col * 32 + src]
                here[place * 4 + s] = pool[s, block]
            for b in range(4):
                here[32 + b] = pool[(z, x)[st], b]

    def arrived(ph):
        for st in range(2):
            for j in range(1, 8):
                second[ph, st, j].wait_recv()

    def right(ph, c):
        here_a, here_b = slots[ph]
        total = None
        for k in range(20):
            e = c * 20 + k
            lhs = jnp.concatenate([here_a[index[e]], here_b[index[80 + e]]], axis=0)
            part = lax.dot_general(lhs, weights[e], (((1,), (1,)), ((), ())), preferred_element_type=F32)
            total = part if total is None else total + part
        return total

    def left(gathered, p):
        total = None
        for k in range(3):
            n = row_nbrs[(2 * y + p) * 3 + k]
            part = jnp.dot(row_weights[p * 3 + k], gathered[n], preferred_element_type=F32)
            total = part if total is None else total + part
        return total

    for ph in range(2):
        for st in range(2):
            for copy in own_pool[ph, st]:
                copy.wait()
        stage_one(ph)
    ys = [
        remote(
            sigma.at[pl.ds(half * 256, 256)],
            gathered_s.at[2 * y + half],
            ys_send.at[half, d - 1],
            ys_recv.at[half, d - 1],
            at(d, 0, 0, 0),
        )
        for half in range(2)
        for d in (1, 3, 2)
    ]
    w_load = [load(col_vals.at[c], weights.at[pl.ds(c * 20, 20)], w_sem.at[c]) for c in range(4)]
    rv_load = [load(row_vals.at[2 * y + p], row_weights.at[pl.ds(p * 3, 3)], rv_sem.at[p]) for p in range(2)]

    stage_two(0)
    stage_two(1)

    for copy in own_s + rv_load:
        copy.wait()
    for copy in ys:
        copy.wait_recv()
    for p in range(2):

        total = left(gathered_s, p).astype(BF16)
        ph = 2 + p
        for st in range(2):
            for b in range(4):
                pools[ph][st][(z, x)[st], b] = total[st * 128 : (st + 1) * 128, b * 256 : (b + 1) * 256]
        stage_one(ph)

    yt = []
    for copy in w_load:
        copy.wait()
    for half in range(2):
        arrived(half)

        def right_t(c, carry, half=half):
            cols = pl.ds(pl.multiple_of(c * 256, 256), 256)
            gathered_t[2 * y + half, :, cols] = right(half, c).astype(BF16)
            return carry

        lax.fori_loop(0, 4, right_t, 0)
        for d in (1, 3, 2):
            yt.append(
                remote(
                    gathered_t.at[2 * y + half],
                    gathered_t.at[2 * y + half],
                    yt_send.at[half, d - 1],
                    yt_recv.at[half, d - 1],
                    at(d, 0, 0, 0),
                )
            )
        stage_two(2 + half)

    for copy in yt:
        copy.wait_recv()
    for p in range(2):

        agg_theta[p] = left(gathered_t, p)

    outs = []
    for half in range(2):
        arrived(2 + half)

        def finish(c, carry, half=half):
            cols = pl.ds(pl.multiple_of(c * 256, 256), 256)
            a = right(2 + half, c)
            scale = jnp.sqrt(var_rows[pl.ds(half * 256, 256), :] * var_cols[:, cols])
            inverse = lax.rsqrt(scale * scale + a * a)
            size = jnp.abs(a)
            angle = arc(jnp.minimum(size, scale) / jnp.maximum(size, scale))
            angle = jnp.where(size > scale, (math.pi / 2) - angle, angle)
            share = 0.5 + jnp.where(a < 0, -angle, angle) * (1 / math.pi)
            kern = scale * (scale * inverse * (1 / math.pi) + share * (a * inverse))
            out_n[half, :, cols] = kern
            out_k[half, :, cols] = kern + agg_theta[half, :, cols] * share
            return carry

        lax.fori_loop(0, 4, finish, 0)
        rows = pl.ds(half * 256, 256)
        outs.append(load(out_n.at[half], nngp.at[rows], out_sem.at[half, 0]))
        outs.append(load(out_k.at[half], ntk.at[rows], out_sem.at[half, 1]))

    for copy in ys + yt:
        copy.wait_send()
    for copy in first.values():
        copy.wait_send()
    for (ph, st, j), copy in second.items():
        if ph >= 2:
            copy.wait_send()
    for copy in outs:
        copy.wait()


def shards(sigma_in, theta_in, var_rows, var_cols, row_nbrs, row_vals, col_nbrs, col_vals):
    rank_col = lax.axis_index("cols")
    entries = col_nbrs.reshape(32, 80)
    owner, within = entries // 4, entries % 4
    want = jnp.max(
        jnp.where(owner[:, None, :] == jnp.arange(32, dtype=jnp.int32)[None, :, None], within[:, None, :], 0), axis=2
    ).reshape(1024)
    mine = lax.dynamic_slice_in_dim(entries, rank_col, 1, 0)[0]
    own, block = mine // 4, mine % 4
    oz, ox, oc = own // 8, (own // 2) % 4, own % 2
    index_a = jnp.where(own == rank_col, 32 + block, (ox * 2 + oc) * 4 + oz)
    index_b = jnp.where(own == rank_col, 32 + block, (oz * 2 + oc) * 4 + ox)
    index = jnp.concatenate([index_a, index_b])

    smem = pl.BlockSpec(memory_space=pltpu.SMEM)
    vmem = pl.BlockSpec(memory_space=pltpu.VMEM)
    hbm = pl.BlockSpec(memory_space=pl.ANY)
    dma = pltpu.SemaphoreType.DMA
    out = jax.ShapeDtypeStruct((512, 1024), F32)
    return pl.pallas_call(
        kernel,
        out_shape=(out, out),
        in_specs=[smem, smem, smem, hbm, hbm, vmem, vmem, hbm, hbm],
        out_specs=(hbm, hbm),
        scratch_shapes=[
            pltpu.VMEM((80, 256, 256), BF16),
            pltpu.VMEM((6, 256, 256), BF16),
            pltpu.VMEM((8, 256, 1024), BF16),
            pltpu.VMEM((8, 256, 1024), BF16),
            pltpu.VMEM((2, 256, 1024), F32),
            pltpu.VMEM((2, 256, 1024), F32),
            pltpu.VMEM((2, 256, 1024), F32),
        ]
        + [pltpu.VMEM((4, 4, 128, 256), BF16)] * 8
        + [pltpu.VMEM((36, 128, 256), BF16)] * 8
        + [pltpu.VMEM((7, 4, 128, 256), BF16)] * 4
        + [
            dma((4,)),
            dma((2,)),
            dma((3, 2, 4)),
            dma((2, 3)),
            dma((2, 3)),
            dma((2, 3)),
            dma((2, 3)),
            dma((4, 2, 3)),
            dma((4, 2, 3)),
            dma((4, 2, 7)),
            dma((4, 2, 7)),
            dma((2, 2)),
        ],
        compiler_params=pltpu.CompilerParams(
            collective_id=0, has_side_effects=True, vmem_limit_bytes=62 * 1024 * 1024
        ),
    )(
        want,
        index,
        row_nbrs.reshape(24),
        theta_in,
        sigma_in,
        var_rows.reshape(512, 1),
        var_cols.reshape(1, 1024),
        row_vals,
        col_vals,
    )


def solution(mesh):
    in_specs = (
        P("rows", "cols"),
        P("rows", "cols"),
        P("rows"),
        P("cols"),
        P(),
        P(),
        P(),
        P("cols", None, None, None),
    )
    out_specs = (P("rows", "cols"), P("rows", "cols"))
    return jax.shard_map(shards, mesh=mesh, in_specs=in_specs, out_specs=out_specs, check_vma=False)
```

time: 592 us -> 164 us (0.28)
  the two profiles are of different devices: /device:TPU:0 before, /device:TPU:1 now
where the time goes in v1:
time: 164 us
  Pallas kernels  153 us (93%)
  local copies, waits for them, and re-layouts  9.06 us (6%)
    pallas_call x1, Pallas kernels, shards(): pl.pallas_call(kernel, out_shape=(out, out), in_specs=[smem, smem, smem,...  153 us
    unnamed x6, local copies, waits for them, and re-layouts  6.2 us

profile of v1, /device:TPU:1, one launch (start us, length us, event | category | flops | bytes accessed | tf_op | source)
XLA Modules:
  0.0 164.3 jit_solution(8880859134166145308)
XLA Ops:
  0.6 0.8 copy.15
  1.4 0.6 reshape.70.row_nbrs
  2.0 0.8 copy.14
  2.8 0.1 reshape.68
  2.9 0.7 pad_add_fusion.index
  3.6 0.6 select_reduce_fusion
  4.2 0.7 reshape.69.want
  4.9 1.5 copy.16.var_rows
  6.4 153.2 %shard_map.95 = (f32[512,1024]{1,0:T(8,128)}, f32[512,1024]{1,0:T(8,128)}) custom-call(s32[1024]{0:T(1024)} %reshape.69.want, s32[160]{0:T(256)} %pad_add_fusion.index, s32[24]{0:T(128)} %reshape.70.row_nbrs, bf16[512,1024]{1,0:T(8,128)(2,1)} %theta.1, bf16[512,1024]{1,0:T(8,128)(2,1)} %sigma.1, f32[512,1]{1,0:T(8,128)} %copy.16.var_rows, ...), custom_call_target="tpu_custom_call" | custom-call | tf_op jit(solution)/shard_map/pallas_call | solution.py:296
  159.6 0.0 copy-start
  159.6 3.3 %copy.19 = f32[512,1024]{1,0:T(8,128)} copy(f32[512,1024]{1,0:T(8,128)} %get-tuple-element.9) | data formatting | bytes 4194304
  163.0 0.0 copy-done
  163.0 1.3 copy.20
  (3 shorter events, 0.1 us)
Async XLA Ops:
  159.6 3.3 %copy-start = (f32[512,1024]{1,0:T(8,128)S(1)}, f32[512,1024]{1,0:T(8,128)}, u32[]{:S(2)}) copy-start(f32[512,1024]{1,0:T(8,128)} %get-tuple-element.10) | copy-start | bytes 6291460

commit v2 on v1

v2 whole, which is shorter than its diff:
```python
import functools
import math

import jax
import jax.numpy as jnp
from jax import lax
from jax.experimental import pallas as pl
from jax.experimental.pallas import tpu as pltpu
from jax.sharding import PartitionSpec as P

MESH = pl.DeviceIdType.MESH
BF16 = jnp.bfloat16
F32 = jnp.float32

ATAN = (
    0.9999998979,
    -0.3333196033,
    0.1996924122,
    -0.1401660921,
    0.09906147193,
    -0.05936764426,
    0.02416647519,
    -0.004668829048,
)


def arc(t):
    t2 = t * t
    total = jnp.full_like(t, ATAN[-1])
    for c in ATAN[-2::-1]:
        total = total * t2 + c
    return total * t


def kernel(
    col_nbrs, row_nbrs, theta, sigma, row_vals, col_vals,
    agg_s, agg_t,
    wanted, weights, row_weights, gathered_s, gathered_t, total_s, total_t,
    pa0, pa1, pa2, pa3, pb0, pb1, pb2, pb3,
    ra0, ra1, ra2, ra3, rb0, rb1, rb2, rb3,
    sa0, sa1, sb0, sb1,
    w_sem, rv_sem, own_sem, ys_send, ys_recv, yt_send, yt_recv,
    one_send, one_recv, two_send, two_recv, out_sem,
):
    pools = ((pa0, pb0), (pa1, pb1), (pa2, pb2), (pa3, pb3))
    slots = ((ra0, rb0), (ra1, rb1), (ra2, rb2), (ra3, rb3))
    sends = ((sa0, sb0), (sa1, sb1), (sa0, sb0), (sa1, sb1))
    y = lax.axis_index("rows")
    col = lax.axis_index("cols")
    z, x, core = col // 8, (col // 2) % 4, col % 2
    mine = (z, x)

    def at(dy, dz, dx, dc):
        return (
            lax.rem(y + dy, 4),
            (lax.rem(z + dz, 4) * 4 + lax.rem(x + dx, 4)) * 2 + lax.rem(core + dc, 2),
        )

    def line(st, d, dc):
        return at(0, d, 0, dc) if st == 0 else at(0, 0, d, dc)

    def local(src, dst, sem):
        copy = pltpu.make_async_copy(src, dst, sem)
        copy.start()
        return copy

    def remote(src, dst, ssem, rsem, device):
        copy = pltpu.make_async_remote_copy(
            src_ref=src, dst_ref=dst, send_sem=ssem, recv_sem=rsem, device_id=device, device_id_type=MESH
        )
        copy.start()
        return copy

    own_pool = [
        local(
            theta.at[pl.ds(ph * 256 + st * 128, 128), pl.ds(b * 256, 256)],
            pools[ph][st].at[mine[st], b],
            own_sem.at[ph, st, b],
        )
        for ph in range(2)
        for st in range(2)
        for b in range(4)
    ]

    barrier = pltpu.get_barrier_semaphore()
    partners = [(dy, 0, 0, 0) for dy in (1, 2, 3)]
    partners += [(0, dz, 0, dc) for dz in (1, 2, 3) for dc in (0, 1)]
    partners += [(0, 0, dx, dc) for dx in (1, 2, 3) for dc in (0, 1)]
    partners += [(0, 0, 0, 1)]
    for p in partners:
        pl.semaphore_signal(barrier, inc=1, device_id=at(*p), device_id_type=MESH)
    pl.semaphore_wait(barrier, len(partners))

    first = {}
    second = {}

    def step(ph, st, way, src, blocks):
        part = pools[ph][st].at[src] if blocks is None else pools[ph][st].at[src, pl.ds(blocks, 2)]
        first[ph, st, way] = remote(
            part, part, one_send.at[ph, st, way], one_recv.at[ph, st, way], line(st, (1, 3)[way % 2], 0)
        )

    def stage_one(ph):
        for st in range(2):
            step(ph, st, 0, mine[st], None)
            step(ph, st, 1, mine[st], None)

    def forward(ph):
        for st in range(2):
            first[ph, st, 0].wait_recv()
            step(ph, st, 2, lax.rem(mine[st] + 3, 4), 0)
        for st in range(2):
            first[ph, st, 1].wait_recv()
            step(ph, st, 3, lax.rem(mine[st] + 1, 4), 2)

    def source_at(st, s):
        return ((s * 4 + x) if st == 0 else (z * 4 + s)) * 2 + core

    def look(st):
        def one(j, carry):
            other = line(1 - st, j // 2, j % 2)[1]
            sources = [source_at(st, s) for s in range(4)]

            def entry(i, found):
                for k in range(20):
                    n = col_nbrs[k, other * 4 + i]
                    owner, block = n // 4, n % 4
                    found = tuple(jnp.where(owner == s, block, f) for s, f in zip(sources, found))
                return found

            found = lax.fori_loop(0, 4, entry, (jnp.int32(0),) * 4)
            for s in range(4):
                wanted[(st * 8 + j) * 4 + s] = found[s]
            return carry

        lax.fori_loop(0, 8, one, 0)

    def stage_two(ph):
        for st in range(2):
            first[ph, st, 2].wait_recv()
            first[ph, st, 3].wait_recv()
            pool, out, here = pools[ph][st], sends[ph][st], slots[ph][st]
            place = mine[1 - st] * 2 + core
            if ph >= 2:
                for j in range(1, 8):
                    second[ph - 2, st, j].wait_send()

            def pack(i, carry):
                j, s = i // 4 + 1, i % 4
                out[j - 1, s] = pool[s, wanted[(st * 8 + j) * 4 + s]]
                return carry

            lax.fori_loop(0, 28, pack, 0)
            for j in (2, 3, 6, 7, 4, 5, 1):
                second[ph, st, j] = remote(
                    out.at[j - 1],
                    here.at[pl.ds(place * 4, 4)],
                    two_send.at[ph, st, j - 1],
                    two_recv.at[ph, st, j - 1],
                    line(1 - st, j // 2, j % 2),
                )
        for st in range(2):
            pool, here = pools[ph][st], slots[ph][st]
            place = mine[1 - st] * 2 + core
            for s in range(4):
                here[place * 4 + s] = pool[s, wanted[st * 32 + s]]
            for b in range(4):
                here[32 + b] = pool[mine[st], b]

    def arrived(ph):
        for st in range(2):
            for j in range(1, 8):
                second[ph, st, j].wait_recv()

    def right(ph, c):
        here_a, here_b = slots[ph]
        total = None
        for k in range(20):
            n = col_nbrs[k, col * 4 + c]
            owner, block = n // 4, n % 4
            oz, ox, oc = owner // 8, (owner // 2) % 4, owner % 2
            index_a = jnp.where(owner == col, 32 + block, (ox * 2 + oc) * 4 + oz)
            index_b = jnp.where(owner == col, 32 + block, (oz * 2 + oc) * 4 + ox)
            lhs = jnp.concatenate([here_a[index_a], here_b[index_b]], axis=0)
            part = lax.dot_general(
                lhs, weights[c * 20 + k], (((1,), (1,)), ((), ())), preferred_element_type=F32
            )
            total = part if total is None else total + part
        return total

    def left(gathered, p):
        total = None
        for k in range(3):
            n = row_nbrs[k, 2 * y + p]
            part = jnp.dot(row_weights[p * 3 + k], gathered[n], preferred_element_type=F32)
            total = part if total is None else total + part
        return total

    for copy in own_pool:
        copy.wait()
    for ph in range(2):
        stage_one(ph)
    ys = [
        remote(
            sigma.at[pl.ds(half * 256, 256)],
            gathered_s.at[2 * y + half],
            ys_send.at[half, d - 1],
            ys_recv.at[half, d - 1],
            at(d, 0, 0, 0),
        )
        for half in range(2)
        for d in (1, 3, 2)
    ]
    loads = [
        local(sigma.at[pl.ds(half * 256, 256)], gathered_s.at[2 * y + half], own_sem.at[2, half, 0])
        for half in range(2)
    ]
    loads += [local(row_vals.at[2 * y + p], row_weights.at[pl.ds(p * 3, 3)], rv_sem.at[p]) for p in range(2)]
    loads += [local(col_vals.at[c], weights.at[pl.ds(c * 20, 20)], w_sem.at[c]) for c in range(4)]

    look(0)
    look(1)
    forward(0)
    forward(1)
    stage_two(0)
    stage_two(1)

    for copy in loads:
        copy.wait()
    for copy in ys:
        copy.wait_recv()
    for p in range(2):
        panel = left(gathered_s, p).astype(BF16)
        for st in range(2):
            for b in range(4):
                pools[2 + p][st][mine[st], b] = panel[st * 128 : (st + 1) * 128, b * 256 : (b + 1) * 256]
        stage_one(2 + p)

    yt = []

    def right_theta(half):
        arrived(half)

        def one(c, carry):
            cols = pl.ds(pl.multiple_of(c * 256, 256), 256)
            gathered_t[2 * y + half, :, cols] = right(half, c).astype(BF16)
            return carry

        lax.fori_loop(0, 4, one, 0)
        for d in (1, 3, 2):
            yt.append(
                remote(
                    gathered_t.at[2 * y + half],
                    gathered_t.at[2 * y + half],
                    yt_send.at[half, d - 1],
                    yt_recv.at[half, d - 1],
                    at(d, 0, 0, 0),
                )
            )

    right_theta(0)
    forward(2)
    forward(3)
    stage_two(2)
    right_theta(1)
    stage_two(3)

    for copy in yt:
        copy.wait_recv()
    outs = []
    for p in range(2):
        total_t[p] = left(gathered_t, p)
        outs.append(local(total_t.at[p], agg_t.at[pl.ds(p * 256, 256)], out_sem.at[p, 0]))

    for half in range(2):
        arrived(2 + half)

        def finish(c, carry, half=half):
            cols = pl.ds(pl.multiple_of(c * 256, 256), 256)
            total_s[half, :, cols] = right(2 + half, c)
            return carry

        lax.fori_loop(0, 4, finish, 0)
        outs.append(local(total_s.at[half], agg_s.at[pl.ds(half * 256, 256)], out_sem.at[half, 1]))

    for copy in ys + yt:
        copy.wait_send()
    for copy in first.values():
        copy.wait_send()
    for (ph, st, j), copy in second.items():
        if ph >= 2:
            copy.wait_send()
    for copy in outs:
        copy.wait()


def update(agg_s, agg_t, var_rows, var_cols, nngp, ntk):
    rows = agg_s.shape[0]
    place = [lax.broadcasted_iota(jnp.int32, (rows, rows), i) for i in range(2)]
    at_rows = jnp.sum(jnp.where(place[0] == place[1], var_rows[...], 0.0), axis=1, keepdims=True)
    a = agg_s[...]
    scale = jnp.sqrt(at_rows * var_cols[...])
    inverse = lax.rsqrt(scale * scale + a * a)
    size = jnp.abs(a)
    angle = arc(jnp.minimum(size, scale) / jnp.maximum(size, scale))
    angle = jnp.where(size > scale, (math.pi / 2) - angle, angle)
    share = 0.5 + jnp.where(a < 0, -angle, angle) * (1 / math.pi)
    kern = scale * (scale * inverse * (1 / math.pi) + share * (a * inverse))
    nngp[...] = kern
    ntk[...] = kern + agg_t[...] * share


def shards(sigma_in, theta_in, var_rows, var_cols, row_nbrs, row_vals, col_nbrs, col_vals):
    smem = pl.BlockSpec(memory_space=pltpu.SMEM)
    hbm = pl.BlockSpec(memory_space=pl.ANY)
    dma = pltpu.SemaphoreType.DMA
    out = jax.ShapeDtypeStruct((512, 1024), F32)
    agg_s, agg_t = pl.pallas_call(
        kernel,
        out_shape=(out, out),
        in_specs=[smem, smem, hbm, hbm, hbm, hbm],
        out_specs=(hbm, hbm),
        scratch_shapes=[
            pltpu.SMEM((64,), jnp.int32),
            pltpu.VMEM((80, 256, 256), BF16),
            pltpu.VMEM((6, 256, 256), BF16),
            pltpu.VMEM((8, 256, 1024), BF16),
            pltpu.VMEM((8, 256, 1024), BF16),
            pltpu.VMEM((2, 256, 1024), F32),
            pltpu.VMEM((2, 256, 1024), F32),
        ]
        + [pltpu.VMEM((4, 4, 128, 256), BF16)] * 8
        + [pltpu.VMEM((36, 128, 256), BF16)] * 8
        + [pltpu.VMEM((7, 4, 128, 256), BF16)] * 4
        + [
            dma((4,)),
            dma((2,)),
            dma((3, 2, 4)),
            dma((2, 3)),
            dma((2, 3)),
            dma((2, 3)),
            dma((2, 3)),
            dma((4, 2, 4)),
            dma((4, 2, 4)),
            dma((4, 2, 7)),
            dma((4, 2, 7)),
            dma((2, 2)),
        ],
        compiler_params=pltpu.CompilerParams(
            collective_id=0, has_side_effects=True, vmem_limit_bytes=62 * 1024 * 1024
        ),
    )(col_nbrs.T, row_nbrs.T, theta_in, sigma_in, row_vals, col_vals)

    rows = 128
    block = pl.BlockSpec((rows, 1024), lambda i: (i, 0))
    return pl.pallas_call(
        update,
        grid=(512 // rows,),
        out_shape=(out, out),
        in_specs=[
            block,
            block,
            pl.BlockSpec((1, rows), lambda i: (0, i)),
            pl.BlockSpec((1, 1024), lambda i: (0, 0)),
        ],
        out_specs=(block, block),
        compiler_params=pltpu.CompilerParams(vmem_limit_bytes=62 * 1024 * 1024),
    )(agg_s, agg_t, var_rows.reshape(1, 512), var_cols.reshape(1, 1024))


def solution(mesh):
    in_specs = (
        P("rows", "cols"),
        P("rows", "cols"),
        P("rows"),
        P("cols"),
        P(),
        P(),
        P(),
        P("cols", None, None, None),
    )
    out_specs = (P("rows", "cols"), P("rows", "cols"))
    return jax.shard_map(shards, mesh=mesh, in_specs=in_specs, out_specs=out_specs, check_vma=False)
```

time: 164 us -> 151 us (0.921)
  local copies, waits for them, and re-layouts: 9.06 us -> 0 us
  Pallas kernels: 153 us -> 150 us
    unnamed x6 -> x0, local copies, waits for them, and re-layouts: 6.2 us -> none
    reshape x4 -> x0, local copies, waits for them, and re-layouts: 2.86 us -> none  [the longest x1 1.53 us: shards(): var_rows.reshape(512, 1)]
    pallas_call x1 -> x2, Pallas kernels: 153 us -> 150 us  [the longest x1 142 us: shards(): pl.pallas_call(kernel, out_shape=(out, out), in_specs=[smem, smem, hbm, h...]
where the time goes in v2:
time: 151 us
  Pallas kernels  150 us (99%)
    pallas_call x1, Pallas kernels, shards(): pl.pallas_call(kernel, out_shape=(out, out), in_specs=[smem, smem, hbm, h...  142 us
    pallas_call x1, Pallas kernels, shards(): pl.pallas_call(update, grid=(512 // rows,), out_shape=(out, out), in_spec...  8.52 us

profile of v2, /device:TPU:1, one launch (start us, length us, event | category | flops | bytes accessed | tf_op | source)
XLA Modules:
  0.0 151.1 jit_solution(9783998879167911900)
XLA Ops:
  0.6 142.0 %shard_map.95 = (f32[512,1024]{1,0:T(8,128)}, f32[512,1024]{1,0:T(8,128)}) custom-call(s32[20,128]{1,0:T(8,128)} %bitcast.4, s32[3,8]{1,0:T(4,128)} %bitcast.6, bf16[512,1024]{1,0:T(8,128)(2,1)} %theta.1, bf16[512,1024]{1,0:T(8,128)(2,1)} %sigma.1, bf16[8,3,256,256]{3,2,1,0:T(8,128)(2,1)} %row_vals.1, bf16[4,20,256,256]{3,2,1,0:T(8,128)(2,1)} %col_vals.1), custom_call_target="tpu_custom_call" | custom-call | tf_op jit(solution)/shard_map/pallas_call | solution.py:318
  142.6 8.5 %shard_map.96 = (f32[512,1024]{1,0:T(8,128)}, f32[512,1024]{1,0:T(8,128)}) custom-call(f32[512,1024]{1,0:T(8,128)} %get-tuple-element.4.agg_s, f32[512,1024]{1,0:T(8,128)} %get-tuple-element.5.agg_t, f32[1,512]{1,0:T(1,128)} %bitcast.7, f32[1,1024]{1,0:T(1,128)} %bitcast.5), custom_call_target="tpu_custom_call" | custom-call | tf_op jit(solution)/shard_map/pallas_call | solution.py:356

commit v3 on v2

v3 whole, which is shorter than its diff:
```python
import functools
import math

import jax
import jax.numpy as jnp
from jax import lax
from jax.experimental import pallas as pl
from jax.experimental.pallas import tpu as pltpu
from jax.sharding import PartitionSpec as P

MESH = pl.DeviceIdType.MESH
BF16 = jnp.bfloat16
F32 = jnp.float32

ATAN = (
    0.9999998979,
    -0.3333196033,
    0.1996924122,
    -0.1401660921,
    0.09906147193,
    -0.05936764426,
    0.02416647519,
    -0.004668829048,
)


INNER = ((0, 0), (0, 1), (0, 3), (1, 1), (3, 3), (2, 1))
HOPS = ((0, (0, 1)), (0, (0, 3)), (1, (1, 0)), (2, (3, 0)), (3, (1, 0)))
OUTER = (((1, 0), (2,)), ((3, 0), (4, 0, 1)), ((0, 1), (1, 3, 5)), ((0, 3), (3, 5, 4)))
PARTS = []
for way, places in OUTER:
    for flip in (0, 1):
        PARTS.append((way, flip, places, sum(len(p[2]) for p in PARTS)))
PARTS.append(((0, 0), 1, (0, 1, 2, 3, 4, 5), 20))
PARTS.append(((0, 0), 0, (1, 2, 3, 4, 5), 26))
OWN = 31
SLOTS = 35


def slot_table():
    table = {}
    for way, flip, places, start in PARTS:
        for i, p in enumerate(places):
            offset = tuple((a + b) % 4 for a, b in zip(INNER[p], way))
            table[offset, flip] = start + i
    table[(0, 0), 0] = OWN
    return table


def arc(t):
    t2 = t * t
    total = jnp.full_like(t, ATAN[-1])
    for c in ATAN[-2::-1]:
        total = total * t2 + c
    return total * t


def kernel(
    col_nbrs, row_nbrs, theta, sigma, row_vals, col_vals,
    agg_s, agg_t,
    wanted, table, weights, row_weights, gathered_s, gathered_t, total,
    pa0, pa1, pa2, pa3, pb0, pb1, pb2, pb3,
    fa0, fa1, fa2, fa3, fb0, fb1, fb2, fb3,
    ra0, ra1, ra2, ra3, rb0, rb1, rb2, rb3,
    sa0, sa1, sb0, sb1,
    w_sem, rv_sem, own_sem, ys_send, ys_recv, yt_send, yt_recv,
    one_send, one_recv, two_send, two_recv, out_sem,
):
    pools = ((pa0, pb0), (pa1, pb1), (pa2, pb2), (pa3, pb3))
    fars = ((fa0, fb0), (fa1, fb1), (fa2, fb2), (fa3, fb3))
    slots = ((ra0, rb0), (ra1, rb1), (ra2, rb2), (ra3, rb3))
    sends = ((sa0, sb0), (sa1, sb1), (sa0, sb0), (sa1, sb1))
    y = lax.axis_index("rows")
    col = lax.axis_index("cols")
    z, x, core = col // 8, (col // 2) % 4, col % 2

    def at(dy, dz, dx, dc):
        return (
            lax.rem(y + dy, 4),
            (lax.rem(z + dz, 4) * 4 + lax.rem(x + dx, 4)) * 2 + lax.rem(core + dc, 2),
        )

    def toward(st, way, flip):
        return at(0, way[st], way[1 - st], flip)

    def local(src, dst, sem):
        copy = pltpu.make_async_copy(src, dst, sem)
        copy.start()
        return copy

    def remote(src, dst, ssem, rsem, device):
        copy = pltpu.make_async_remote_copy(
            src_ref=src, dst_ref=dst, send_sem=ssem, recv_sem=rsem, device_id=device, device_id_type=MESH
        )
        copy.start()
        return copy

    own_pool = [
        local(
            theta.at[pl.ds(ph * 256 + st * 128, 128), pl.ds(b * 256, 256)],
            pools[ph][st].at[0, b],
            own_sem.at[ph, st, b],
        )
        for ph in range(2)
        for st in range(2)
        for b in range(4)
    ]

    barrier = pltpu.get_barrier_semaphore()
    partners = [(dy, 0, 0, 0) for dy in (1, 2, 3)] + [(0, 0, 0, 1)]
    partners += [(0, d, 0, dc) for d in (1, 3) for dc in (0, 1)]
    partners += [(0, 0, d, dc) for d in (1, 3) for dc in (0, 1)]
    for p in partners:
        pl.semaphore_signal(barrier, inc=1, device_id=at(*p), device_id_type=MESH)
    pl.semaphore_wait(barrier, len(partners))

    first = {}
    second = {}

    def held(ph, st, place):
        return fars[ph][st] if place == 5 else pools[ph][st].at[place]

    def chosen(ph, st, place, block):
        return fars[ph][st][block] if place == 5 else pools[ph][st][place, block]

    def hop(ph, i):
        for st in range(2):
            src, way = HOPS[i]
            if src:
                first[ph, st, src - 1].wait_recv()
            first[ph, st, i] = remote(
                held(ph, st, src), held(ph, st, i + 1), one_send.at[ph, st, i], one_recv.at[ph, st, i], toward(st, way, 0)
            )

    def hop_one(ph):
        hop(ph, 0)
        hop(ph, 1)

    def hop_two(ph):
        hop(ph, 2)
        hop(ph, 3)

    def look(parts):
        for m in parts:
            for st in range(2):
                way, flip, places, start = PARTS[m]
                other = toward(st, way, flip)[1]
                sources = [toward(st, tuple((4 - o) % 4 for o in INNER[place]), 0)[1] for place in places]

                def entry(i, found, other=other, sources=sources):
                    for k in range(20):
                        n = col_nbrs[k, other * 4 + i]
                        owner, block = n // 4, n % 4
                        found = tuple(jnp.where(owner == s, block, f) for s, f in zip(sources, found))
                    return found

                found = lax.fori_loop(0, 4, entry, (jnp.int32(0),) * len(places))
                for i, f in enumerate(found):
                    wanted[st * 32 + start + i] = f

    def serve(ph, parts):
        for st in range(2):
            out, here = sends[ph][st], slots[ph][st]
            for m in parts:
                way, flip, places, start = PARTS[m]
                if ph >= 2:
                    second[ph - 2, st, m].wait_send()
                for i, place in enumerate(places):
                    out[start + i] = chosen(ph, st, place, wanted[st * 32 + start + i])
                part = pl.ds(start, len(places))
                second[ph, st, m] = remote(
                    out.at[part], here.at[part], two_send.at[ph, st, m], two_recv.at[ph, st, m], toward(st, way, flip)
                )

    def serve_one(ph):
        for st in range(2):
            first[ph, st, 3].wait_recv()
        serve(ph, (2, 3, 0, 1))

    def serve_two(ph):
        for st in range(2):
            first[ph, st, 4].wait_recv()
        serve(ph, (4, 6, 5, 7, 8))
        for st in range(2):
            here = slots[ph][st]
            for i, place in enumerate(PARTS[9][2]):
                here[PARTS[9][3] + i] = chosen(ph, st, place, wanted[st * 32 + PARTS[9][3] + i])
            for b in range(4):
                here[OWN + b] = pools[ph][st][0, b]

    def arrived(ph):
        for st in range(2):
            for m in range(9):
                second[ph, st, m].wait_recv()

    def right(ph, c):
        here_a, here_b = slots[ph]
        total = None
        for k in range(20):
            n = col_nbrs[k, col * 4 + c]
            owner, block = n // 4, n % 4
            extra = jnp.where(owner == col, block, 0)
            index_a = table[owner] + extra
            index_b = table[32 + owner] + extra
            lhs = jnp.concatenate([here_a[index_a], here_b[index_b]], axis=0)
            part = lax.dot_general(
                lhs, weights[c * 20 + k], (((1,), (1,)), ((), ())), preferred_element_type=F32
            )
            total = part if total is None else total + part
        return total

    def left(gathered, p):
        total = None
        for k in range(3):
            n = row_nbrs[k, 2 * y + p]
            part = jnp.dot(row_weights[p * 3 + k], gathered[n], preferred_element_type=F32)
            total = part if total is None else total + part
        return total

    for copy in own_pool:
        copy.wait()
    hop_one(0)
    hop_one(1)
    ys = [
        remote(
            sigma.at[pl.ds(half * 256, 256)],
            gathered_s.at[2 * y + half],
            ys_send.at[half, d - 1],
            ys_recv.at[half, d - 1],
            at(d, 0, 0, 0),
        )
        for half in range(2)
        for d in (1, 3, 2)
    ]
    loads = [
        local(sigma.at[pl.ds(half * 256, 256)], gathered_s.at[2 * y + half], own_sem.at[2, half, 0])
        for half in range(2)
    ]
    loads += [local(row_vals.at[2 * y + p], row_weights.at[pl.ds(p * 3, 3)], rv_sem.at[p]) for p in range(2)]
    loads += [local(col_vals.at[c], weights.at[pl.ds(c * 20, 20)], w_sem.at[c]) for c in range(4)]

    look((0, 1, 2, 3))
    hop_two(0)
    look((4, 5, 6, 7))
    hop_two(1)
    hop(0, 4)
    serve_one(0)
    hop(1, 4)
    serve_one(1)
    look((8, 9))
    serve_two(0)
    serve_two(1)

    slot_of = slot_table()
    for dz in range(4):
        for dx in range(4):
            for flip in range(2):
                owner = at(0, (4 - dz) % 4, (4 - dx) % 4, flip)[1]
                table[owner] = slot_of[(dz, dx), flip]
                table[32 + owner] = slot_of[(dx, dz), flip]

    for copy in loads:
        copy.wait()
    for copy in ys:
        copy.wait_recv()
    for p in range(2):
        panel = left(gathered_s, p).astype(BF16)
        for st in range(2):
            for b in range(4):
                pools[2 + p][st][0, b] = panel[st * 128 : (st + 1) * 128, b * 256 : (b + 1) * 256]
        hop_one(2 + p)

    yt = []

    def right_theta(half):
        arrived(half)

        def one(c, carry):
            cols = pl.ds(pl.multiple_of(c * 256, 256), 256)
            gathered_t[2 * y + half, :, cols] = right(half, c).astype(BF16)
            return carry

        lax.fori_loop(0, 4, one, 0)
        for d in (1, 3, 2):
            yt.append(
                remote(
                    gathered_t.at[2 * y + half],
                    gathered_t.at[2 * y + half],
                    yt_send.at[half, d - 1],
                    yt_recv.at[half, d - 1],
                    at(d, 0, 0, 0),
                )
            )

    right_theta(0)
    hop_two(2)
    hop_two(3)
    hop(2, 4)
    serve_one(2)
    hop(3, 4)
    serve_one(3)
    serve_two(2)
    right_theta(1)
    serve_two(3)

    for copy in yt:
        copy.wait_recv()
    outs = []
    for p in range(2):
        total[p] = left(gathered_t, p)
        outs.append(local(total.at[p], agg_t.at[pl.ds(p * 256, 256)], out_sem.at[p, 0]))

    for half in range(2):
        arrived(2 + half)
        outs[half].wait()

        def finish(c, carry, half=half):
            cols = pl.ds(pl.multiple_of(c * 256, 256), 256)
            total[half, :, cols] = right(2 + half, c)
            return carry

        lax.fori_loop(0, 4, finish, 0)
        outs.append(local(total.at[half], agg_s.at[pl.ds(half * 256, 256)], out_sem.at[half, 1]))

    for copy in ys + yt:
        copy.wait_send()
    for copy in first.values():
        copy.wait_send()
    for (ph, st, j), copy in second.items():
        if ph >= 2:
            copy.wait_send()
    for copy in outs[2:]:
        copy.wait()


def update(agg_s, agg_t, var_rows, var_cols, nngp, ntk, s_in, t_in, n_out, k_out, in_sem, out_sem):
    rows = 64
    parts = 512 // rows
    loads = []
    for i in range(parts):
        for j, (src, dst) in enumerate(((agg_s, s_in), (agg_t, t_in))):
            copy = pltpu.make_async_copy(src.at[pl.ds(i * rows, rows)], dst.at[i], in_sem.at[i, j])
            copy.start()
            loads.append(copy)
    place = [lax.broadcasted_iota(jnp.int32, (128, 128), i) for i in range(2)]
    scale_cols = jnp.sqrt(var_cols[...])
    stores = []
    for i in range(parts):
        at, lane = i * rows % 128, i * rows // 128 * 128
        spread = jnp.where(place[0] == place[1], var_rows[:, lane : lane + 128], 0.0)[at : at + rows]
        scale = jnp.sqrt(jnp.sum(spread, axis=1, keepdims=True)) * scale_cols
        loads[2 * i].wait()
        loads[2 * i + 1].wait()
        a = s_in[i]
        square = scale * scale + a * a
        inverse = lax.rsqrt(square)
        angle = arc(a / (scale + square * inverse))
        share = 0.5 + angle * (2 / math.pi)
        kern = scale * (scale * inverse * (1 / math.pi) + share * (a * inverse))
        n_out[i] = kern
        k_out[i] = kern + t_in[i] * share
        for j, (src, dst) in enumerate(((n_out, nngp), (k_out, ntk))):
            copy = pltpu.make_async_copy(src.at[i], dst.at[pl.ds(i * rows, rows)], out_sem.at[i, j])
            copy.start()
            stores.append(copy)
    for copy in stores:
        copy.wait()


def shards(sigma_in, theta_in, var_rows, var_cols, row_nbrs, row_vals, col_nbrs, col_vals):
    smem = pl.BlockSpec(memory_space=pltpu.SMEM)
    hbm = pl.BlockSpec(memory_space=pl.ANY)
    dma = pltpu.SemaphoreType.DMA
    out = jax.ShapeDtypeStruct((512, 1024), F32)
    agg_s, agg_t = pl.pallas_call(
        kernel,
        out_shape=(out, out),
        in_specs=[smem, smem, hbm, hbm, hbm, hbm],
        out_specs=(hbm, hbm),
        scratch_shapes=[
            pltpu.SMEM((64,), jnp.int32),
            pltpu.SMEM((64,), jnp.int32),
            pltpu.VMEM((80, 256, 256), BF16),
            pltpu.VMEM((6, 256, 256), BF16),
            pltpu.VMEM((8, 256, 1024), BF16),
            pltpu.VMEM((8, 256, 1024), BF16),
            pltpu.VMEM((2, 256, 1024), F32),
        ]
        + [pltpu.VMEM((5, 4, 128, 256), BF16)] * 8
        + [pltpu.VMEM((4, 128, 256), BF16)] * 8
        + [pltpu.VMEM((SLOTS, 128, 256), BF16)] * 8
        + [pltpu.VMEM((26, 128, 256), BF16)] * 4
        + [
            dma((4,)),
            dma((2,)),
            dma((3, 2, 4)),
            dma((2, 3)),
            dma((2, 3)),
            dma((2, 3)),
            dma((2, 3)),
            dma((4, 2, 5)),
            dma((4, 2, 5)),
            dma((4, 2, 9)),
            dma((4, 2, 9)),
            dma((2, 2)),
        ],
        compiler_params=pltpu.CompilerParams(
            collective_id=0, has_side_effects=True, vmem_limit_bytes=62 * 1024 * 1024
        ),
    )(col_nbrs.T, row_nbrs.T, theta_in, sigma_in, row_vals, col_vals)

    vmem = pl.BlockSpec(memory_space=pltpu.VMEM)
    return pl.pallas_call(
        update,
        out_shape=(out, out),
        in_specs=[hbm, hbm, vmem, vmem],
        out_specs=(hbm, hbm),
        scratch_shapes=[pltpu.VMEM((8, 64, 1024), F32)] * 4 + [dma((8, 2)), dma((8, 2))],
        compiler_params=pltpu.CompilerParams(vmem_limit_bytes=62 * 1024 * 1024),
    )(agg_s, agg_t, var_rows.reshape(1, 512), var_cols.reshape(1, 1024))


def solution(mesh):
    in_specs = (
        P("rows", "cols"),
        P("rows", "cols"),
        P("rows"),
        P("cols"),
        P(),
        P(),
        P(),
        P("cols", None, None, None),
    )
    out_specs = (P("rows", "cols"), P("rows", "cols"))
    return jax.shard_map(shards, mesh=mesh, in_specs=in_specs, out_specs=out_specs, check_vma=False)
```

time: 151 us -> 143 us (0.947)
  Pallas kernels: 150 us -> 141 us
    pallas_call x1, Pallas kernels: 142 us -> 135 us  [shards(): pl.pallas_call(kernel, out_shape=(out, out), in_specs=[smem, smem, hbm, h...]
    pallas_call x1, Pallas kernels: 8.52 us -> 6.48 us  [shards(): pl.pallas_call(update, out_shape=(out, out), in_specs=[hbm, hbm, vmem, vm...]
where the time goes in v3:
time: 143 us; the launch traced here: 142 us
  Pallas kernels  141 us (99%)
    pallas_call x1, Pallas kernels, shards(): pl.pallas_call(kernel, out_shape=(out, out), in_specs=[smem, smem, hbm, h...  135 us
    pallas_call x1, Pallas kernels, shards(): pl.pallas_call(update, out_shape=(out, out), in_specs=[hbm, hbm, vmem, vm...  6.48 us

profile of v3, /device:TPU:1, one launch (start us, length us, event | category | flops | bytes accessed | tf_op | source)
XLA Modules:
  0.0 142.3 jit_solution(1994282488540819225)
XLA Ops:
  0.6 135.0 %shard_map.95 = (f32[512,1024]{1,0:T(8,128)}, f32[512,1024]{1,0:T(8,128)}) custom-call(s32[20,128]{1,0:T(8,128)} %bitcast.4, s32[3,8]{1,0:T(4,128)} %bitcast.6, bf16[512,1024]{1,0:T(8,128)(2,1)} %theta.1, bf16[512,1024]{1,0:T(8,128)(2,1)} %sigma.1, bf16[8,3,256,256]{3,2,1,0:T(8,128)(2,1)} %row_vals.1, bf16[4,20,256,256]{3,2,1,0:T(8,128)(2,1)} %col_vals.1), custom_call_target="tpu_custom_call" | custom-call | tf_op jit(solution)/shard_map/pallas_call | solution.py:375
  135.6 6.5 %shard_map.96 = (f32[512,1024]{1,0:T(8,128)}, f32[512,1024]{1,0:T(8,128)}) custom-call(f32[512,1024]{1,0:T(8,128)} %get-tuple-element.4.agg_s, f32[512,1024]{1,0:T(8,128)} %get-tuple-element.5.agg_t, f32[1,512]{1,0:T(1,128)} %bitcast.7, f32[1,1024]{1,0:T(1,128)} %bitcast.5), custom_call_target="tpu_custom_call" | custom-call | tf_op jit(solution)/shard_map/pallas_call | solution.py:413

commit v4 on v3

--- a/solution.py
+++ b/solution.py
@@ -58,7 +58,7 @@
 def kernel(
     col_nbrs, row_nbrs, theta, sigma, row_vals, col_vals,
     agg_s, agg_t,
-    wanted, table, weights, row_weights, gathered_s, gathered_t, total,
+    wanted, table, weights, row_weights, gathered_s, gathered_t, total_s, total_t,
     pa0, pa1, pa2, pa3, pb0, pb1, pb2, pb3,
     fa0, fa1, fa2, fa3, fb0, fb1, fb2, fb3,
     ra0, ra1, ra2, ra3, rb0, rb1, rb2, rb3,
@@ -245,10 +245,10 @@
     hop_two(1)
     hop(0, 4)
     serve_one(0)
+    look((8, 9))
+    serve_two(0)
     hop(1, 4)
     serve_one(1)
-    look((8, 9))
-    serve_two(0)
     serve_two(1)
 
     slot_of = slot_table()
@@ -295,32 +295,34 @@
     right_theta(0)
     hop_two(2)
     hop_two(3)
+    right_theta(1)
     hop(2, 4)
     serve_one(2)
+    serve_two(2)
     hop(3, 4)
     serve_one(3)
-    serve_two(2)
-    right_theta(1)
     serve_two(3)
 
+    outs = []
+
+    def right_sigma(half):
+        arrived(2 + half)
+
+        def one(c, carry):
+            cols = pl.ds(pl.multiple_of(c * 256, 256), 256)
+            total_s[half, :, cols] = right(2 + half, c)
+            return carry
+
+        lax.fori_loop(0, 4, one, 0)
+        outs.append(local(total_s.at[half], agg_s.at[pl.ds(half * 256, 256)], out_sem.at[half, 1]))
+
+    right_sigma(0)
     for copy in yt:
         copy.wait_recv()
-    outs = []
     for p in range(2):
-        total[p] = left(gathered_t, p)
-        outs.append(local(total.at[p], agg_t.at[pl.ds(p * 256, 256)], out_sem.at[p, 0]))
-
-    for half in range(2):
-        arrived(2 + half)
-        outs[half].wait()
-
-        def finish(c, carry, half=half):
-            cols = pl.ds(pl.multiple_of(c * 256, 256), 256)
-            total[half, :, cols] = right(2 + half, c)
-            return carry
-
-        lax.fori_loop(0, 4, finish, 0)
-        outs.append(local(total.at[half], agg_s.at[pl.ds(half * 256, 256)], out_sem.at[half, 1]))
+        total_t[p] = left(gathered_t, p)
+        outs.append(local(total_t.at[p], agg_t.at[pl.ds(p * 256, 256)], out_sem.at[p, 0]))
+    right_sigma(1)
 
     for copy in ys + yt:
         copy.wait_send()
@@ -329,7 +331,7 @@
     for (ph, st, j), copy in second.items():
         if ph >= 2:
             copy.wait_send()
-    for copy in outs[2:]:
+    for copy in outs:
         copy.wait()
 
 
@@ -385,6 +387,7 @@
             pltpu.VMEM((8, 256, 1024), BF16),
             pltpu.VMEM((8, 256, 1024), BF16),
             pltpu.VMEM((2, 256, 1024), F32),
+            pltpu.VMEM((2, 256, 1024), F32),
         ]
         + [pltpu.VMEM((5, 4, 128, 256), BF16)] * 8
         + [pltpu.VMEM((4, 128, 256), BF16)] * 8

time: 143 us -> 137 us (0.958)
  Pallas kernels: 141 us -> 136 us
    pallas_call x1, Pallas kernels: 135 us -> 129 us  [shards(): pl.pallas_call(kernel, out_shape=(out, out), in_specs=[smem, smem, hbm, h...]
where the time goes in v4:
time: 137 us
  Pallas kernels  136 us (99%)
    pallas_call x1, Pallas kernels, shards(): pl.pallas_call(kernel, out_shape=(out, out), in_specs=[smem, smem, hbm, h...  129 us
    pallas_call x1, Pallas kernels, shards(): pl.pallas_call(update, out_shape=(out, out), in_specs=[hbm, hbm, vmem, vm...  6.48 us

profile of v4, /device:TPU:1, one launch (start us, length us, event | category | flops | bytes accessed | tf_op | source)
XLA Modules:
  0.0 136.6 jit_solution(9241252046068211410)
XLA Ops:
  0.6 129.3 %shard_map.95 = (f32[512,1024]{1,0:T(8,128)}, f32[512,1024]{1,0:T(8,128)}) custom-call(s32[20,128]{1,0:T(8,128)} %bitcast.4, s32[3,8]{1,0:T(4,128)} %bitcast.6, bf16[512,1024]{1,0:T(8,128)(2,1)} %theta.1, bf16[512,1024]{1,0:T(8,128)(2,1)} %sigma.1, bf16[8,3,256,256]{3,2,1,0:T(8,128)(2,1)} %row_vals.1, bf16[4,20,256,256]{3,2,1,0:T(8,128)(2,1)} %col_vals.1), custom_call_target="tpu_custom_call" | custom-call | tf_op jit(solution)/shard_map/pallas_call | solution.py:377
  130.0 6.5 %shard_map.96 = (f32[512,1024]{1,0:T(8,128)}, f32[512,1024]{1,0:T(8,128)}) custom-call(f32[512,1024]{1,0:T(8,128)} %get-tuple-element.4.agg_s, f32[512,1024]{1,0:T(8,128)} %get-tuple-element.5.agg_t, f32[1,512]{1,0:T(1,128)} %bitcast.7, f32[1,1024]{1,0:T(1,128)} %bitcast.5), custom_call_target="tpu_custom_call" | custom-call | tf_op jit(solution)/shard_map/pallas_call | solution.py:416

commit v5 on v4

--- a/solution.py
+++ b/solution.py
@@ -26,13 +26,14 @@
 
 INNER = ((0, 0), (0, 1), (0, 3), (1, 1), (3, 3), (2, 1))
 HOPS = ((0, (0, 1)), (0, (0, 3)), (1, (1, 0)), (2, (3, 0)), (3, (1, 0)))
-OUTER = (((1, 0), (2,)), ((3, 0), (4, 0, 1)), ((0, 1), (1, 3, 5)), ((0, 3), (3, 5, 4)))
+OUTER = (((1, 0), (2,)), ((3, 0), (4, 0, 1)), ((0, 1), (1, 3)), ((0, 3), (3, 4)), ((0, 1), (5,)), ((0, 3), (5,)))
 PARTS = []
 for way, places in OUTER:
     for flip in (0, 1):
         PARTS.append((way, flip, places, sum(len(p[2]) for p in PARTS)))
 PARTS.append(((0, 0), 1, (0, 1, 2, 3, 4, 5), 20))
 PARTS.append(((0, 0), 0, (1, 2, 3, 4, 5), 26))
+SIBLING, SELF = 12, 13
 OWN = 31
 SLOTS = 35
 
@@ -55,10 +56,24 @@
     return total * t
 
 
+def column(row):
+    place = [lax.broadcasted_iota(jnp.int32, (128, 128), i) for i in range(2)]
+    return jnp.sum(jnp.where(place[0] == place[1], row, 0.0), axis=1, keepdims=True)
+
+
+def both(a, t, scale):
+    square = scale * scale + a * a
+    inverse = lax.rsqrt(square)
+    angle = arc(a / (scale + square * inverse))
+    share = 0.5 + angle * (2 / math.pi)
+    kern = scale * (scale * inverse * (1 / math.pi) + share * (a * inverse))
+    return kern, kern + t * share
+
+
 def kernel(
-    col_nbrs, row_nbrs, theta, sigma, row_vals, col_vals,
-    agg_s, agg_t,
-    wanted, table, weights, row_weights, gathered_s, gathered_t, total_s, total_t,
+    col_nbrs, row_nbrs, var_rows, var_cols, theta, sigma, row_vals, col_vals,
+    part_s, part_t,
+    wanted, table, index, weights, row_weights, gathered_s, gathered_t, total_s, total_t,
     pa0, pa1, pa2, pa3, pb0, pb1, pb2, pb3,
     fa0, fa1, fa2, fa3, fb0, fb1, fb2, fb3,
     ra0, ra1, ra2, ra3, rb0, rb1, rb2, rb3,
@@ -140,23 +155,27 @@
         hop(ph, 2)
         hop(ph, 3)
 
-    def look(parts):
-        for m in parts:
-            for st in range(2):
-                way, flip, places, start = PARTS[m]
-                other = toward(st, way, flip)[1]
-                sources = [toward(st, tuple((4 - o) % 4 for o in INNER[place]), 0)[1] for place in places]
-
-                def entry(i, found, other=other, sources=sources):
-                    for k in range(20):
-                        n = col_nbrs[k, other * 4 + i]
-                        owner, block = n // 4, n % 4
-                        found = tuple(jnp.where(owner == s, block, f) for s, f in zip(sources, found))
-                    return found
-
-                found = lax.fori_loop(0, 4, entry, (jnp.int32(0),) * len(places))
-                for i, f in enumerate(found):
-                    wanted[st * 32 + start + i] = f
+    def look(way, flip):
+        jobs = []
+        for st in range(2):
+            for there, f, places, start in PARTS:
+                if (there[st], there[1 - st]) == way and f == flip:
+                    jobs += [
+                        (st * 32 + start + i, toward(st, tuple((4 - o) % 4 for o in INNER[place]), 0)[1])
+                        for i, place in enumerate(places)
+                    ]
+        other = at(0, way[0], way[1], flip)[1]
+
+        def entry(i, found):
+            for k in range(20):
+                n = col_nbrs[k, other * 4 + i]
+                owner, block = n // 4, n % 4
+                found = tuple(jnp.where(owner == j[1], block, f) for j, f in zip(jobs, found))
+            return found
+
+        found = lax.fori_loop(0, 4, entry, (jnp.int32(0),) * len(jobs))
+        for j, f in zip(jobs, found):
+            wanted[j[0]] = f
 
     def serve(ph, parts):
         for st in range(2):
@@ -175,37 +194,32 @@
     def serve_one(ph):
         for st in range(2):
             first[ph, st, 3].wait_recv()
-        serve(ph, (2, 3, 0, 1))
+        serve(ph, (2, 3, 4, 5, 6, 7, 0, 1))
 
     def serve_two(ph):
         for st in range(2):
             first[ph, st, 4].wait_recv()
-        serve(ph, (4, 6, 5, 7, 8))
+        serve(ph, (8, 10, 9, 11, SIBLING))
         for st in range(2):
             here = slots[ph][st]
-            for i, place in enumerate(PARTS[9][2]):
-                here[PARTS[9][3] + i] = chosen(ph, st, place, wanted[st * 32 + PARTS[9][3] + i])
+            start = PARTS[SELF][3]
+            for i, place in enumerate(PARTS[SELF][2]):
+                here[start + i] = chosen(ph, st, place, wanted[st * 32 + start + i])
             for b in range(4):
                 here[OWN + b] = pools[ph][st][0, b]
 
     def arrived(ph):
         for st in range(2):
-            for m in range(9):
+            for m in range(SIBLING + 1):
                 second[ph, st, m].wait_recv()
 
     def right(ph, c):
         here_a, here_b = slots[ph]
         total = None
         for k in range(20):
-            n = col_nbrs[k, col * 4 + c]
-            owner, block = n // 4, n % 4
-            extra = jnp.where(owner == col, block, 0)
-            index_a = table[owner] + extra
-            index_b = table[32 + owner] + extra
-            lhs = jnp.concatenate([here_a[index_a], here_b[index_b]], axis=0)
-            part = lax.dot_general(
-                lhs, weights[c * 20 + k], (((1,), (1,)), ((), ())), preferred_element_type=F32
-            )
+            e = c * 20 + k
+            lhs = jnp.concatenate([here_a[index[e]], here_b[index[80 + e]]], axis=0)
+            part = lax.dot_general(lhs, weights[e], (((1,), (1,)), ((), ())), preferred_element_type=F32)
             total = part if total is None else total + part
         return total
 
@@ -239,13 +253,18 @@
     loads += [local(row_vals.at[2 * y + p], row_weights.at[pl.ds(p * 3, 3)], rv_sem.at[p]) for p in range(2)]
     loads += [local(col_vals.at[c], weights.at[pl.ds(c * 20, 20)], w_sem.at[c]) for c in range(4)]
 
-    look((0, 1, 2, 3))
+    for way in ((1, 0), (0, 1)):
+        for flip in range(2):
+            look(way, flip)
     hop_two(0)
-    look((4, 5, 6, 7))
+    for way in ((3, 0), (0, 3)):
+        for flip in range(2):
+            look(way, flip)
     hop_two(1)
     hop(0, 4)
     serve_one(0)
-    look((8, 9))
+    for flip in range(2):
+        look((0, 0), flip)
     serve_two(0)
     hop(1, 4)
     serve_one(1)
@@ -258,6 +277,17 @@
                 owner = at(0, (4 - dz) % 4, (4 - dx) % 4, flip)[1]
                 table[owner] = slot_of[(dz, dx), flip]
                 table[32 + owner] = slot_of[(dx, dz), flip]
+
+    def place_of(c, carry):
+        for k in range(20):
+            n = col_nbrs[k, col * 4 + c]
+            owner, block = n // 4, n % 4
+            extra = jnp.where(owner == col, block, 0)
+            index[c * 20 + k] = table[owner] + extra
+            index[80 + c * 20 + k] = table[32 + owner] + extra
+        return carry
+
+    lax.fori_loop(0, 4, place_of, 0)
 
     for copy in loads:
         copy.wait()
@@ -305,24 +335,52 @@
 
     outs = []
 
-    def right_sigma(half):
-        arrived(2 + half)
-
-        def one(c, carry):
-            cols = pl.ds(pl.multiple_of(c * 256, 256), 256)
-            total_s[half, :, cols] = right(2 + half, c)
-            return carry
-
-        lax.fori_loop(0, 4, one, 0)
-        outs.append(local(total_s.at[half], agg_s.at[pl.ds(half * 256, 256)], out_sem.at[half, 1]))
-
-    right_sigma(0)
+    def write(src, dst, rows, cols, sem):
+        return pltpu.make_async_copy(src, dst.at[rows, cols], sem)
+
+    top, low = pl.ds(0, 256), pl.ds(256, 256)
+
+    arrived(2)
+
+    def right_top(c, carry):
+        total_s[0, c] = right(2, c)
+        return carry
+
+    lax.fori_loop(0, 4, right_top, 0)
     for copy in yt:
         copy.wait_recv()
     for p in range(2):
-        total_t[p] = left(gathered_t, p)
-        outs.append(local(total_t.at[p], agg_t.at[pl.ds(p * 256, 256)], out_sem.at[p, 0]))
-    right_sigma(1)
+        both_cols = left(gathered_t, p)
+        for c in range(4):
+            total_t[p, c] = both_cols[:, c * 256 : (c + 1) * 256]
+    scale_rows = jnp.sqrt(jnp.concatenate([column(var_rows[:, 0:128]), column(var_rows[:, 128:256])], axis=0))
+
+    def finish(c, carry):
+        cols = pl.ds(pl.multiple_of(c * 256, 256), 256)
+        scale = scale_rows * jnp.sqrt(var_cols[:, cols])
+        total_s[0, c], total_t[0, c] = both(total_s[0, c], total_t[0, c], scale)
+        return carry
+
+    lax.fori_loop(0, 4, finish, 0)
+    for c in range(4):
+        cols = pl.ds(c * 256, 256)
+        outs.append(write(total_s.at[0, c], part_s, top, cols, out_sem.at[0, c]))
+        outs.append(write(total_t.at[0, c], part_t, top, cols, out_sem.at[1, c]))
+        outs.append(write(total_t.at[1, c], part_t, low, cols, out_sem.at[2, c]))
+    for copy in outs:
+        copy.start()
+
+    arrived(3)
+
+    def right_low(c, carry):
+        cols = pl.ds(pl.multiple_of(c * 256, 256), 256)
+        total_s[1, c] = right(3, c)
+        write(total_s.at[1, c], part_s, low, cols, out_sem.at[3, c]).start()
+        return carry
+
+    lax.fori_loop(0, 4, right_low, 0)
+    for c in range(4):
+        outs.append(write(total_s.at[1, c], part_s, low, pl.ds(c * 256, 256), out_sem.at[3, c]))
 
     for copy in ys + yt:
         copy.wait_send()
@@ -335,36 +393,43 @@
         copy.wait()
 
 
-def update(agg_s, agg_t, var_rows, var_cols, nngp, ntk, s_in, t_in, n_out, k_out, in_sem, out_sem):
-    rows = 64
-    parts = 512 // rows
+def update(var_rows, var_cols, part_s, part_t, nngp, ntk, s_in, t_in, n_out, k_out, s_top, t_top, in_sem, out_sem, top_in, top_out):
+    rows = 32
+    parts = 256 // rows
     loads = []
     for i in range(parts):
-        for j, (src, dst) in enumerate(((agg_s, s_in), (agg_t, t_in))):
-            copy = pltpu.make_async_copy(src.at[pl.ds(i * rows, rows)], dst.at[i], in_sem.at[i, j])
-            copy.start()
-            loads.append(copy)
-    place = [lax.broadcasted_iota(jnp.int32, (128, 128), i) for i in range(2)]
+        for j, (src, dst) in enumerate(((part_s, s_in), (part_t, t_in))):
+            loads.append(pltpu.make_async_copy(src.at[pl.ds(256 + i * rows, rows)], dst.at[i], in_sem.at[i, j]))
+    tops, stores = [], []
+    for i in range(2):
+        for j, (src, mid, dst) in enumerate(((part_s, s_top, nngp), (part_t, t_top, ntk))):
+            here = pl.ds(i * 128, 128)
+            tops.append(
+                (
+                    pltpu.make_async_copy(src.at[here], mid.at[i], top_in.at[i, j]),
+                    pltpu.make_async_copy(mid.at[i], dst.at[here], top_out.at[i, j]),
+                )
+            )
+    for copy in loads:
+        copy.start()
+    for copy, _ in tops:
+        copy.start()
     scale_cols = jnp.sqrt(var_cols[...])
-    stores = []
     for i in range(parts):
-        at, lane = i * rows % 128, i * rows // 128 * 128
-        spread = jnp.where(place[0] == place[1], var_rows[:, lane : lane + 128], 0.0)[at : at + rows]
-        scale = jnp.sqrt(jnp.sum(spread, axis=1, keepdims=True)) * scale_cols
+        first, lane = i * rows % 128, 256 + i * rows // 128 * 128
+        scale = jnp.sqrt(column(var_rows[:, lane : lane + 128])[first : first + rows]) * scale_cols
         loads[2 * i].wait()
         loads[2 * i + 1].wait()
-        a = s_in[i]
-        square = scale * scale + a * a
-        inverse = lax.rsqrt(square)
-        angle = arc(a / (scale + square * inverse))
-        share = 0.5 + angle * (2 / math.pi)
-        kern = scale * (scale * inverse * (1 / math.pi) + share * (a * inverse))
-        n_out[i] = kern
-        k_out[i] = kern + t_in[i] * share
+        n_out[i], k_out[i] = both(s_in[i], t_in[i], scale)
         for j, (src, dst) in enumerate(((n_out, nngp), (k_out, ntk))):
-            copy = pltpu.make_async_copy(src.at[i], dst.at[pl.ds(i * rows, rows)], out_sem.at[i, j])
+            copy = pltpu.make_async_copy(src.at[i], dst.at[pl.ds(256 + i * rows, rows)], out_sem.at[i, j])
             copy.start()
             stores.append(copy)
+        if i % 2 and i // 2 < len(tops):
+            there, back = tops[i // 2]
+            there.wait()
+            back.start()
+            stores.append(back)
     for copy in stores:
         copy.wait()
 
@@ -374,20 +439,23 @@
     hbm = pl.BlockSpec(memory_space=pl.ANY)
     dma = pltpu.SemaphoreType.DMA
     out = jax.ShapeDtypeStruct((512, 1024), F32)
-    agg_s, agg_t = pl.pallas_call(
+    vmem = pl.BlockSpec(memory_space=pltpu.VMEM)
+    var_rows, var_cols = var_rows.reshape(1, 512), var_cols.reshape(1, 1024)
+    part_s, part_t = pl.pallas_call(
         kernel,
         out_shape=(out, out),
-        in_specs=[smem, smem, hbm, hbm, hbm, hbm],
+        in_specs=[smem, smem, vmem, vmem, hbm, hbm, hbm, hbm],
         out_specs=(hbm, hbm),
         scratch_shapes=[
             pltpu.SMEM((64,), jnp.int32),
             pltpu.SMEM((64,), jnp.int32),
+            pltpu.SMEM((160,), jnp.int32),
             pltpu.VMEM((80, 256, 256), BF16),
             pltpu.VMEM((6, 256, 256), BF16),
             pltpu.VMEM((8, 256, 1024), BF16),
             pltpu.VMEM((8, 256, 1024), BF16),
-            pltpu.VMEM((2, 256, 1024), F32),
-            pltpu.VMEM((2, 256, 1024), F32),
+            pltpu.VMEM((2, 4, 256, 256), F32),
+            pltpu.VMEM((2, 4, 256, 256), F32),
         ]
         + [pltpu.VMEM((5, 4, 128, 256), BF16)] * 8
         + [pltpu.VMEM((4, 128, 256), BF16)] * 8
@@ -403,24 +471,25 @@
             dma((2, 3)),
             dma((4, 2, 5)),
             dma((4, 2, 5)),
-            dma((4, 2, 9)),
-            dma((4, 2, 9)),
-            dma((2, 2)),
+            dma((4, 2, 13)),
+            dma((4, 2, 13)),
+            dma((4, 4)),
         ],
         compiler_params=pltpu.CompilerParams(
             collective_id=0, has_side_effects=True, vmem_limit_bytes=62 * 1024 * 1024
         ),
-    )(col_nbrs.T, row_nbrs.T, theta_in, sigma_in, row_vals, col_vals)
-
-    vmem = pl.BlockSpec(memory_space=pltpu.VMEM)
+    )(col_nbrs.T, row_nbrs.T, var_rows, var_cols, theta_in, sigma_in, row_vals, col_vals)
+
     return pl.pallas_call(
         update,
         out_shape=(out, out),
-        in_specs=[hbm, hbm, vmem, vmem],
+        in_specs=[vmem, vmem, hbm, hbm],
         out_specs=(hbm, hbm),
-        scratch_shapes=[pltpu.VMEM((8, 64, 1024), F32)] * 4 + [dma((8, 2)), dma((8, 2))],
+        scratch_shapes=[pltpu.VMEM((8, 32, 1024), F32)] * 4
+        + [pltpu.VMEM((2, 128, 1024), F32)] * 2
+        + [dma((8, 2)), dma((8, 2)), dma((2, 2)), dma((2, 2))],
         compiler_params=pltpu.CompilerParams(vmem_limit_bytes=62 * 1024 * 1024),
-    )(agg_s, agg_t, var_rows.reshape(1, 512), var_cols.reshape(1, 1024))
+    )(var_rows, var_cols, part_s, part_t)
 
 
 def solution(mesh):

time: 137 us -> 135 us (0.985)
  Pallas kernels: 136 us -> 134 us
    pallas_call x2, Pallas kernels: 136 us -> 134 us  [the longest x1 130 us: shards(): pl.pallas_call(kernel, out_shape=(out, out), in_specs=[smem, smem, vmem,...]
where the time goes in v5:
time: 135 us
  Pallas kernels  134 us (99%)
    pallas_call x1, Pallas kernels, shards(): pl.pallas_call(kernel, out_shape=(out, out), in_specs=[smem, smem, vmem,...  130 us
    pallas_call x1, Pallas kernels, shards(): pl.pallas_call(update, out_shape=(out, out), in_specs=[vmem, vmem, hbm, h...  4.92 us

profile of v5, /device:TPU:1, one launch (start us, length us, event | category | flops | bytes accessed | tf_op | source)
XLA Modules:
  0.0 135.1 jit_solution(16402204481445239181)
XLA Ops:
  0.6 129.5 %shard_map.95 = (f32[512,1024]{1,0:T(8,128)}, f32[512,1024]{1,0:T(8,128)}) custom-call(s32[20,128]{1,0:T(8,128)} %bitcast.6, s32[3,8]{1,0:T(4,128)} %bitcast.9, f32[1,512]{1,0:T(1,128)} %bitcast.7, f32[1,1024]{1,0:T(1,128)} %bitcast.4, bf16[512,1024]{1,0:T(8,128)(2,1)} %theta.1, bf16[512,1024]{1,0:T(8,128)(2,1)} %sigma.1, bf16[8,3,256,256]{3,2,1,0:T(8,128)(2,1)} %row_vals.1, ...), custom_call_target="tpu_custom_call" | custom-call | tf_op jit(solution)/shard_map/pallas_call | solution.py:444
  130.2 4.9 %shard_map.96 = (f32[512,1024]{1,0:T(8,128)}, f32[512,1024]{1,0:T(8,128)}) custom-call(f32[1,512]{1,0:T(1,128)} %bitcast.8, f32[1,1024]{1,0:T(1,128)} %bitcast.5, f32[512,1024]{1,0:T(8,128)} %get-tuple-element.4.part_s, f32[512,1024]{1,0:T(8,128)} %get-tuple-element.5.part_t), custom_call_target="tpu_custom_call" | custom-call | tf_op jit(solution)/shard_map/pallas_call | solution.py:483

commit v6 on v5

--- a/solution.py
+++ b/solution.py
@@ -26,14 +26,14 @@
 
 INNER = ((0, 0), (0, 1), (0, 3), (1, 1), (3, 3), (2, 1))
 HOPS = ((0, (0, 1)), (0, (0, 3)), (1, (1, 0)), (2, (3, 0)), (3, (1, 0)))
-OUTER = (((1, 0), (2,)), ((3, 0), (4, 0, 1)), ((0, 1), (1, 3)), ((0, 3), (3, 4)), ((0, 1), (5,)), ((0, 3), (5,)))
+OUTER = (((1, 0), (2,)), ((3, 0), (4, 0, 1)), ((0, 1), (1, 3, 5)), ((0, 3), (3, 5, 4)))
 PARTS = []
 for way, places in OUTER:
     for flip in (0, 1):
         PARTS.append((way, flip, places, sum(len(p[2]) for p in PARTS)))
 PARTS.append(((0, 0), 1, (0, 1, 2, 3, 4, 5), 20))
 PARTS.append(((0, 0), 0, (1, 2, 3, 4, 5), 26))
-SIBLING, SELF = 12, 13
+SIBLING, SELF = 8, 9
 OWN = 31
 SLOTS = 35
 
@@ -71,15 +71,15 @@
 
 
 def kernel(
-    col_nbrs, row_nbrs, var_rows, var_cols, theta, sigma, row_vals, col_vals,
+    col_hbm, row_nbrs, var_rows_hbm, var_cols_hbm, theta, sigma, row_vals, col_vals,
     part_s, part_t,
-    wanted, table, index, weights, row_weights, gathered_s, gathered_t, total_s, total_t,
+    col_nbrs, var_rows, var_cols, wanted, table, index, weights, row_weights, gathered_s, gathered_t, total_s, total_t,
     pa0, pa1, pa2, pa3, pb0, pb1, pb2, pb3,
     fa0, fa1, fa2, fa3, fb0, fb1, fb2, fb3,
     ra0, ra1, ra2, ra3, rb0, rb1, rb2, rb3,
     sa0, sa1, sb0, sb1,
     w_sem, rv_sem, own_sem, ys_send, ys_recv, yt_send, yt_recv,
-    one_send, one_recv, two_send, two_recv, out_sem,
+    one_send, one_recv, two_send, two_recv, out_sem, small_sem,
 ):
     pools = ((pa0, pb0), (pa1, pb1), (pa2, pb2), (pa3, pb3))
     fars = ((fa0, fb0), (fa1, fb1), (fa2, fb2), (fa3, fb3))
@@ -119,6 +119,11 @@
         for ph in range(2)
         for st in range(2)
         for b in range(4)
+    ]
+
+    smalls = [
+        local(src, dst, small_sem.at[i])
+        for i, (src, dst) in enumerate(((col_hbm, col_nbrs), (var_rows_hbm, var_rows), (var_cols_hbm, var_cols)))
     ]
 
     barrier = pltpu.get_barrier_semaphore()
@@ -194,12 +199,12 @@
     def serve_one(ph):
         for st in range(2):
             first[ph, st, 3].wait_recv()
-        serve(ph, (2, 3, 4, 5, 6, 7, 0, 1))
+        serve(ph, (2, 3, 0, 1))
 
     def serve_two(ph):
         for st in range(2):
             first[ph, st, 4].wait_recv()
-        serve(ph, (8, 10, 9, 11, SIBLING))
+        serve(ph, (4, 6, 5, 7, SIBLING))
         for st in range(2):
             here = slots[ph][st]
             start = PARTS[SELF][3]
@@ -253,6 +258,8 @@
     loads += [local(row_vals.at[2 * y + p], row_weights.at[pl.ds(p * 3, 3)], rv_sem.at[p]) for p in range(2)]
     loads += [local(col_vals.at[c], weights.at[pl.ds(c * 20, 20)], w_sem.at[c]) for c in range(4)]
 
+    for copy in smalls:
+        copy.wait()
     for way in ((1, 0), (0, 1)):
         for flip in range(2):
             look(way, flip)
@@ -263,11 +270,11 @@
     hop_two(1)
     hop(0, 4)
     serve_one(0)
+    hop(1, 4)
+    serve_one(1)
     for flip in range(2):
         look((0, 0), flip)
     serve_two(0)
-    hop(1, 4)
-    serve_one(1)
     serve_two(1)
 
     slot_of = slot_table()
@@ -328,8 +335,8 @@
     right_theta(1)
     hop(2, 4)
     serve_one(2)
+    hop(3, 4)
     serve_two(2)
-    hop(3, 4)
     serve_one(3)
     serve_two(3)
 
@@ -353,12 +360,14 @@
         both_cols = left(gathered_t, p)
         for c in range(4):
             total_t[p, c] = both_cols[:, c * 256 : (c + 1) * 256]
-    scale_rows = jnp.sqrt(jnp.concatenate([column(var_rows[:, 0:128]), column(var_rows[:, 128:256])], axis=0))
+
+    def scale_of(half, cols):
+        parts = [column(var_rows[:, half * 256 + i : half * 256 + i + 128]) for i in (0, 128)]
+        return jnp.sqrt(jnp.concatenate(parts, axis=0)) * jnp.sqrt(var_cols[:, cols])
 
     def finish(c, carry):
         cols = pl.ds(pl.multiple_of(c * 256, 256), 256)
-        scale = scale_rows * jnp.sqrt(var_cols[:, cols])
-        total_s[0, c], total_t[0, c] = both(total_s[0, c], total_t[0, c], scale)
+        total_s[0, c], total_t[0, c] = both(total_s[0, c], total_t[0, c], scale_of(0, cols))
         return carry
 
     lax.fori_loop(0, 4, finish, 0)
@@ -366,21 +375,17 @@
         cols = pl.ds(c * 256, 256)
         outs.append(write(total_s.at[0, c], part_s, top, cols, out_sem.at[0, c]))
         outs.append(write(total_t.at[0, c], part_t, top, cols, out_sem.at[1, c]))
-        outs.append(write(total_t.at[1, c], part_t, low, cols, out_sem.at[2, c]))
     for copy in outs:
         copy.start()
 
     arrived(3)
-
-    def right_low(c, carry):
-        cols = pl.ds(pl.multiple_of(c * 256, 256), 256)
-        total_s[1, c] = right(3, c)
-        write(total_s.at[1, c], part_s, low, cols, out_sem.at[3, c]).start()
-        return carry
-
-    lax.fori_loop(0, 4, right_low, 0)
+    scale_rows = scale_of(1, pl.ds(0, 1024))
     for c in range(4):
-        outs.append(write(total_s.at[1, c], part_s, low, pl.ds(c * 256, 256), out_sem.at[3, c]))
+        cols = pl.ds(c * 256, 256)
+        total_s[1, c], total_t[1, c] = both(right(3, c), total_t[1, c], scale_rows[:, c * 256 : (c + 1) * 256])
+        for i, (src, dst) in enumerate(((total_s, part_s), (total_t, part_t))):
+            outs.append(write(src.at[1, c], dst, low, cols, out_sem.at[2 + i, c]))
+            outs[-1].start()
 
     for copy in ys + yt:
         copy.wait_send()
@@ -393,45 +398,24 @@
         copy.wait()
 
 
-def update(var_rows, var_cols, part_s, part_t, nngp, ntk, s_in, t_in, n_out, k_out, s_top, t_top, in_sem, out_sem, top_in, top_out):
-    rows = 32
-    parts = 256 // rows
-    loads = []
-    for i in range(parts):
-        for j, (src, dst) in enumerate(((part_s, s_in), (part_t, t_in))):
-            loads.append(pltpu.make_async_copy(src.at[pl.ds(256 + i * rows, rows)], dst.at[i], in_sem.at[i, j]))
-    tops, stores = [], []
-    for i in range(2):
-        for j, (src, mid, dst) in enumerate(((part_s, s_top, nngp), (part_t, t_top, ntk))):
-            here = pl.ds(i * 128, 128)
-            tops.append(
+def update(part_s, part_t, nngp, ntk, held, in_sem, out_sem):
+    copies = []
+    for i in range(4):
+        rows = pl.ds(i * 128, 128)
+        for j, (src, dst) in enumerate(((part_s, nngp), (part_t, ntk))):
+            copies.append(
                 (
-                    pltpu.make_async_copy(src.at[here], mid.at[i], top_in.at[i, j]),
-                    pltpu.make_async_copy(mid.at[i], dst.at[here], top_out.at[i, j]),
+                    pltpu.make_async_copy(src.at[rows], held.at[i, j], in_sem.at[i, j]),
+                    pltpu.make_async_copy(held.at[i, j], dst.at[rows], out_sem.at[i, j]),
                 )
             )
-    for copy in loads:
-        copy.start()
-    for copy, _ in tops:
-        copy.start()
-    scale_cols = jnp.sqrt(var_cols[...])
-    for i in range(parts):
-        first, lane = i * rows % 128, 256 + i * rows // 128 * 128
-        scale = jnp.sqrt(column(var_rows[:, lane : lane + 128])[first : first + rows]) * scale_cols
-        loads[2 * i].wait()
-        loads[2 * i + 1].wait()
-        n_out[i], k_out[i] = both(s_in[i], t_in[i], scale)
-        for j, (src, dst) in enumerate(((n_out, nngp), (k_out, ntk))):
-            copy = pltpu.make_async_copy(src.at[i], dst.at[pl.ds(256 + i * rows, rows)], out_sem.at[i, j])
-            copy.start()
-            stores.append(copy)
-        if i % 2 and i // 2 < len(tops):
-            there, back = tops[i // 2]
-            there.wait()
-            back.start()
-            stores.append(back)
-    for copy in stores:
-        copy.wait()
+    for there, _ in copies:
+        there.start()
+    for there, back in copies:
+        there.wait()
+        back.start()
+    for _, back in copies:
+        back.wait()
 
 
 def shards(sigma_in, theta_in, var_rows, var_cols, row_nbrs, row_vals, col_nbrs, col_vals):
@@ -444,9 +428,12 @@
     part_s, part_t = pl.pallas_call(
         kernel,
         out_shape=(out, out),
-        in_specs=[smem, smem, vmem, vmem, hbm, hbm, hbm, hbm],
+        in_specs=[hbm, smem, hbm, hbm, hbm, hbm, hbm, hbm],
         out_specs=(hbm, hbm),
         scratch_shapes=[
+            pltpu.SMEM((20, 128), jnp.int32),
+            pltpu.VMEM((1, 512), F32),
+            pltpu.VMEM((1, 1024), F32),
             pltpu.SMEM((64,), jnp.int32),
             pltpu.SMEM((64,), jnp.int32),
             pltpu.SMEM((160,), jnp.int32),
@@ -471,9 +458,10 @@
             dma((2, 3)),
             dma((4, 2, 5)),
             dma((4, 2, 5)),
-            dma((4, 2, 13)),
-            dma((4, 2, 13)),
+            dma((4, 2, 9)),
+            dma((4, 2, 9)),
             dma((4, 4)),
+            dma((3,)),
         ],
         compiler_params=pltpu.CompilerParams(
             collective_id=0, has_side_effects=True, vmem_limit_bytes=62 * 1024 * 1024
@@ -483,13 +471,11 @@
     return pl.pallas_call(
         update,
         out_shape=(out, out),
-        in_specs=[vmem, vmem, hbm, hbm],
+        in_specs=[hbm, hbm],
         out_specs=(hbm, hbm),
-        scratch_shapes=[pltpu.VMEM((8, 32, 1024), F32)] * 4
-        + [pltpu.VMEM((2, 128, 1024), F32)] * 2
-        + [dma((8, 2)), dma((8, 2)), dma((2, 2)), dma((2, 2))],
+        scratch_shapes=[pltpu.VMEM((4, 2, 128, 1024), F32), dma((4, 2)), dma((4, 2))],
         compiler_params=pltpu.CompilerParams(vmem_limit_bytes=62 * 1024 * 1024),
-    )(var_rows, var_cols, part_s, part_t)
+    )(part_s, part_t)
 
 
 def solution(mesh):

time: 135 us -> 134 us (level)
  no operation moved by 1% of the time
where the time goes in v6:
time: 134 us
  Pallas kernels  133 us (99%)
    pallas_call x1, Pallas kernels, shards(): pl.pallas_call(kernel, out_shape=(out, out), in_specs=[hbm, smem, hbm, hb...  130 us
    pallas_call x1, Pallas kernels, shards(): pl.pallas_call(update, out_shape=(out, out), in_specs=[hbm, hbm], out_spe...  3.58 us

profile of v6, /device:TPU:1, one launch (start us, length us, event | category | flops | bytes accessed | tf_op | source)
XLA Modules:
  0.0 134.0 jit_solution(7482348819807144961)
XLA Ops:
  0.6 129.6 %shard_map.95 = (f32[512,1024]{1,0:T(8,128)}, f32[512,1024]{1,0:T(8,128)}) custom-call(s32[20,128]{1,0:T(8,128)} %bitcast.4, s32[3,8]{1,0:T(4,128)} %bitcast.6, f32[1,512]{1,0:T(1,128)} %bitcast.7, f32[1,1024]{1,0:T(1,128)} %bitcast.5, bf16[512,1024]{1,0:T(8,128)(2,1)} %theta.1, bf16[512,1024]{1,0:T(8,128)(2,1)} %sigma.1, bf16[8,3,256,256]{3,2,1,0:T(8,128)(2,1)} %row_vals.1, ...), custom_call_target="tpu_custom_call" | custom-call | tf_op jit(solution)/shard_map/pallas_call | solution.py:428
  130.2 3.6 %shard_map.96 = (f32[512,1024]{1,0:T(8,128)}, f32[512,1024]{1,0:T(8,128)}) custom-call(f32[512,1024]{1,0:T(8,128)} %get-tuple-element.4.part_s, f32[512,1024]{1,0:T(8,128)} %get-tuple-element.5.part_t), custom_call_target="tpu_custom_call" | custom-call | tf_op jit(solution)/shard_map/pallas_call | solution.py:471

commit v7 on v6

--- a/solution.py
+++ b/solution.py
@@ -183,9 +183,9 @@
             wanted[j[0]] = f
 
     def serve(ph, parts):
-        for st in range(2):
-            out, here = sends[ph][st], slots[ph][st]
-            for m in parts:
+        for m in parts:
+            for st in range(2):
+                out, here = sends[ph][st], slots[ph][st]
                 way, flip, places, start = PARTS[m]
                 if ph >= 2:
                     second[ph - 2, st, m].wait_send()
@@ -236,10 +236,10 @@
             total = part if total is None else total + part
         return total
 
-    for copy in own_pool:
-        copy.wait()
-    hop_one(0)
-    hop_one(1)
+    for ph in range(2):
+        for copy in own_pool[ph * 8 : ph * 8 + 8]:
+            copy.wait()
+        hop_one(ph)
     ys = [
         remote(
             sigma.at[pl.ds(half * 256, 256)],
@@ -400,8 +400,8 @@
 
 def update(part_s, part_t, nngp, ntk, held, in_sem, out_sem):
     copies = []
-    for i in range(4):
-        rows = pl.ds(i * 128, 128)
+    for i in range(2):
+        rows = pl.ds(i * 256, 256)
         for j, (src, dst) in enumerate(((part_s, nngp), (part_t, ntk))):
             copies.append(
                 (
@@ -473,7 +473,7 @@
         out_shape=(out, out),
         in_specs=[hbm, hbm],
         out_specs=(hbm, hbm),
-        scratch_shapes=[pltpu.VMEM((4, 2, 128, 1024), F32), dma((4, 2)), dma((4, 2))],
+        scratch_shapes=[pltpu.VMEM((2, 2, 256, 1024), F32), dma((2, 2)), dma((2, 2))],
         compiler_params=pltpu.CompilerParams(vmem_limit_bytes=62 * 1024 * 1024),
     )(part_s, part_t)
 

time: 134 us -> 134 us (level)
  no operation moved by 1% of the time
where the time goes in v7:
time: 134 us
  Pallas kernels  133 us (99%)
    pallas_call x1, Pallas kernels, shards(): pl.pallas_call(kernel, out_shape=(out, out), in_specs=[hbm, smem, hbm, hb...  130 us
    pallas_call x1, Pallas kernels, shards(): pl.pallas_call(update, out_shape=(out, out), in_specs=[hbm, hbm], out_spe...  3.3 us

profile of v7, /device:TPU:1, one launch (start us, length us, event | category | flops | bytes accessed | tf_op | source)
XLA Modules:
  0.0 133.7 jit_solution(14267953768414193773)
XLA Ops:
  0.6 129.6 %shard_map.95 = (f32[512,1024]{1,0:T(8,128)}, f32[512,1024]{1,0:T(8,128)}) custom-call(s32[20,128]{1,0:T(8,128)} %bitcast.4, s32[3,8]{1,0:T(4,128)} %bitcast.6, f32[1,512]{1,0:T(1,128)} %bitcast.7, f32[1,1024]{1,0:T(1,128)} %bitcast.5, bf16[512,1024]{1,0:T(8,128)(2,1)} %theta.1, bf16[512,1024]{1,0:T(8,128)(2,1)} %sigma.1, bf16[8,3,256,256]{3,2,1,0:T(8,128)(2,1)} %row_vals.1, ...), custom_call_target="tpu_custom_call" | custom-call | tf_op jit(solution)/shard_map/pallas_call | solution.py:428
  130.2 3.3 %shard_map.96 = (f32[512,1024]{1,0:T(8,128)}, f32[512,1024]{1,0:T(8,128)}) custom-call(f32[512,1024]{1,0:T(8,128)} %get-tuple-element.4.part_s, f32[512,1024]{1,0:T(8,128)} %get-tuple-element.5.part_t), custom_call_target="tpu_custom_call" | custom-call | tf_op jit(solution)/shard_map/pallas_call | solution.py:471
